TPU v7x, 512 devices: a whole 4x8x8 slice. The times are simulated.
512 devices in a mesh: seq: 32 (over y_hi, x, core), dp: 16 (over z, y_lo).
Axes of the slice: x: 4, y: 8 (y_hi: 4, y_lo: 2; y = y_hi * 2 + y_lo), z: 8, core: 2. Of those that a mesh axis runs over, the one named last changes fastest.
Arguments:
- hidden_in: bfloat16 [16, 4096, 8192], P('dp', 'seq'), may hold values from -6 to 6
- queries: bfloat16 [16, 4096, 4096], P('dp', 'seq'), may hold values from -512 to 512
- keys: bfloat16 [16, 4096, 1024], P('dp', 'seq'), may hold values from -4 to 4
- values: bfloat16 [16, 4096, 1024], P('dp', 'seq'), may hold values from -6 to 6
- out_grad: bfloat16 [16, 4096, 4096], P('dp', 'seq'), may hold values from -6 to 6
- doc_ids: int32 [16, 4096], P('dp', 'seq'), may hold values from 0 to 63, never falling along the last dimension, each value on 1 to 128 neighbouring positions
- projection: bfloat16 [8192, 256], P('dp'), may hold values from -0.0625 to 0.0625
- mom1_q: float32 [256, 4096], P('dp', 'seq'), may hold values from -18 to 18
- mom2_q: float32 [256, 4096], P('dp', 'seq'), may hold values from 4 to 400
- mom1_kv: float32 [2, 256, 1024], P(None, 'dp', 'seq'), may hold values from -18 to 18
- mom2_kv: float32 [2, 256, 1024], P(None, 'dp', 'seq'), may hold values from 4 to 400
Outputs:
- new_mom1_q: float32 [256, 4096], P('dp', 'seq')
- new_mom2_q: float32 [256, 4096], P('dp', 'seq')
- update_q: float32 [256, 4096], P('dp', 'seq')
- new_mom1_kv: float32 [2, 256, 1024], P(None, 'dp', 'seq')
- new_mom2_kv: float32 [2, 256, 1024], P(None, 'dp', 'seq')
- update_kv: float32 [2, 256, 1024], P(None, 'dp', 'seq')
Inputs may be any that keep to these rules, and one draw needn't show every extreme that they name: `doc_ids`: document ids never fall along a replica's positions, and one document holds at most 128 positions.
All inputs are finite; a program needn't handle non-finite values.
Results may differ from a plain program's by a relative error of at most 0.019.
Values may be sent and summed in bfloat16 or wider, within the bound.
A program may use at most 128 MiB of HBM per device.

v0:
```python
import jax
import jax.numpy as jnp
from jax import lax
from jax.sharding import PartitionSpec as P

H = 32
KVH = 8
HD = 128
QBLK = 512
DOC_CAP = 128
ADAM_STEP = 100


beta_first = 0.9
beta_second = 0.999
adam_epsilon = 1e-08


def from_partner(value, axis, stride):
    return lax.ppermute(value, axis, [(i, i ^ 1 << stride) for i in range(lax.axis_size(axis))])


def contract_first(left_side, right_side):
    return lax.dot_general(
        left_side, right_side, (((0,), (0,)), ((), ())), preferred_element_type=jnp.float32
    )


def make_windows(rows_in, band):
    pieces = rows_in.reshape((rows_in.shape[0] // band, band) + rows_in.shape[1:])
    before = jnp.concatenate(
        [jnp.zeros((1,) + pieces.shape[1:], pieces.dtype), pieces[:-1]], axis=0
    )
    return (pieces, jnp.concatenate([before, pieces], axis=1))


def head_grads(query, keyset, valueset, outgrad, documents, band):
    length, width = query.shape
    score_scale = 1.0 / width**0.5
    per_block = QBLK // band
    query_sub = query.reshape(length // band, band, width)
    grad_sub = outgrad.reshape(length // band, band, width)
    unused_keys, key_win = make_windows(keyset, band)
    unused_values, value_win = make_windows(valueset, band)
    doc_sub = documents.reshape(length // band, band)
    doc_before = jnp.concatenate([jnp.full((1, band), -1, jnp.int32), doc_sub[:-1]], axis=0)
    doc_win = jnp.concatenate([doc_before, doc_sub], axis=1)
    row_place = jnp.arange(band)
    col_place = jnp.arange(2 * band)
    causal = col_place[None, :] <= row_place[:, None] + band
    query_parts = []
    key_parts = []
    value_parts = []
    for block_index in range(length // QBLK):
        low = block_index * per_block
        top = low + per_block
        query_block = query_sub[low:top]
        grad_block = grad_sub[low:top]
        keys_seen = key_win[low:top]
        values_seen = value_win[low:top]
        scores = (
            jnp.einsum("sqd,skd->sqk", query_block, keys_seen, preferred_element_type=jnp.float32)
            * score_scale
        )
        visible = causal[None, :, :] & (
            doc_win[low:top][:, None, :] == doc_sub[low:top][:, :, None]
        )
        masked = jnp.where(visible, scores, -jnp.inf)
        row_peak = jnp.max(masked, axis=2, keepdims=True)
        weights = jnp.exp(masked - row_peak)
        attention = weights / jnp.sum(weights, axis=2, keepdims=True)
        attention_low = attention.astype(jnp.bfloat16)
        output = jnp.einsum(
            "sqk,skd->sqd", attention_low, values_seen, preferred_element_type=jnp.float32
        )
        row_delta = jnp.sum(grad_block.astype(jnp.float32) * output, axis=2, keepdims=True)
        grad_attention = jnp.einsum(
            "sqd,skd->sqk", grad_block, values_seen, preferred_element_type=jnp.float32
        )
        grad_scores = (attention * (grad_attention - row_delta)).astype(jnp.bfloat16)
        query_parts.append(
            (
                jnp.einsum(
                    "sqk,skd->sqd", grad_scores, keys_seen, preferred_element_type=jnp.float32
                )
                * score_scale
            ).astype(jnp.bfloat16)
        )
        key_parts.append(
            jnp.einsum("sqk,sqd->skd", grad_scores, query_block, preferred_element_type=jnp.float32)
            * score_scale
        )
        value_parts.append(
            jnp.einsum(
                "sqk,sqd->skd", attention_low, grad_block, preferred_element_type=jnp.float32
            )
        )

    def fold_windows(parts):
        whole = jnp.concatenate(parts, axis=0)
        later = jnp.concatenate(
            [whole[1:, :band], jnp.zeros((1, band, width), jnp.float32)], axis=0
        )
        return (whole[:, band:] + later).reshape(length, width).astype(jnp.bfloat16)

    return (
        jnp.concatenate(query_parts, axis=0).reshape(length, width),
        fold_windows(key_parts),
        fold_windows(value_parts),
    )


def adam_update(first_moment, second_moment, gradient):
    first_new = beta_first * first_moment + (1.0 - beta_first) * gradient
    second_new = beta_second * second_moment + (1.0 - beta_second) * gradient * gradient
    corrected_first = first_new / (1.0 - beta_first**ADAM_STEP)
    corrected_second = second_new / (1.0 - beta_second**ADAM_STEP)
    return (first_new, second_new, corrected_first / (jnp.sqrt(corrected_second) + adam_epsilon))


def on_device(
    hidden_in,
    queries,
    keys,
    values,
    out_grad,
    doc_ids,
    projection,
    mom1_q,
    mom2_q,
    mom1_kv,
    mom2_kv,
):
    seq_devices = lax.axis_size("seq")
    local_heads = H // seq_devices
    group_size = H // KVH
    group_span = max(1, group_size // local_heads)
    key_local = max(1, local_heads // group_size)
    span_bits = group_span.bit_length() - 1
    token_rows = hidden_in.shape[1]
    full_length = token_rows * seq_devices
    band = min(DOC_CAP, full_length // 4)
    device_index = lax.axis_index("seq")
    hidden_rows = hidden_in[0]
    rank_width = projection.shape[1]
    lowrank = jnp.dot(
        hidden_rows,
        lax.all_gather(projection, "dp", axis=0, tiled=True),
        preferred_element_type=jnp.float32,
    ).astype(jnp.bfloat16)
    documents = lax.all_gather(doc_ids[0], "seq", axis=0, tiled=True)
    query_rows = queries[0]
    grad_rows = out_grad[0]
    key_rows = jnp.repeat(keys[0].reshape(token_rows, KVH, HD), group_size, axis=1).reshape(
        token_rows, H * HD
    )
    value_rows = jnp.repeat(values[0].reshape(token_rows, KVH, HD), group_size, axis=1).reshape(
        token_rows, H * HD
    )
    query_heads, grad_heads, key_heads, value_heads = (
        lax.all_to_all(query_rows, "seq", split_axis=1, concat_axis=0, tiled=True),
        lax.all_to_all(grad_rows, "seq", split_axis=1, concat_axis=0, tiled=True),
        lax.all_to_all(key_rows, "seq", split_axis=1, concat_axis=0, tiled=True),
        lax.all_to_all(value_rows, "seq", split_axis=1, concat_axis=0, tiled=True),
    )
    grad_query, grad_key, grad_value = head_grads(
        query_heads, key_heads, value_heads, grad_heads, documents, band
    )
    query_grads = [grad_query]
    key_grads = [grad_key]
    value_grads = [grad_value]
    gradients = jnp.concatenate(query_grads + key_grads + value_grads, axis=1)
    projected = contract_first(lax.all_gather(lowrank, "seq", axis=0, tiled=True), gradients)
    width_query = local_heads * HD

    def group_heads(block_cols):
        return (
            block_cols.reshape(rank_width, key_local, local_heads // key_local, HD)
            .sum(axis=2)
            .reshape(rank_width, key_local * HD)
        )

    query_terms = projected[:, :width_query]
    pair_terms = jnp.stack(
        [
            group_heads(projected[:, width_query : 2 * width_query]),
            group_heads(projected[:, 2 * width_query :]),
        ]
    )
    block_cols = pair_terms
    for bit_index in reversed(range(span_bits)):
        half_width = block_cols.shape[2] // 2
        upper_half = device_index >> bit_index & 1 == 1
        kept_half = jnp.where(
            upper_half, block_cols[:, :, half_width:], block_cols[:, :, :half_width]
        )
        sent_half = jnp.where(
            upper_half, block_cols[:, :, :half_width], block_cols[:, :, half_width:]
        )
        block_cols = kept_half + from_partner(sent_half, "seq", bit_index)
    query_shard, pair_shard = (
        lax.psum_scatter(query_terms, "dp", scatter_dimension=0, tiled=True),
        lax.psum_scatter(block_cols, "dp", scatter_dimension=1, tiled=True),
    )
    first_query, second_query, update_query = adam_update(mom1_q, mom2_q, query_shard)
    first_pair, second_pair, update_pair = adam_update(mom1_kv, mom2_kv, pair_shard)
    return (first_query, second_query, update_query, first_pair, second_pair, update_pair)


def solution(mesh):
    in_specs = (
        P("dp", "seq", None),
        P("dp", "seq", None),
        P("dp", "seq", None),
        P("dp", "seq", None),
        P("dp", "seq", None),
        P("dp", "seq"),
        P("dp", None),
        P("dp", "seq"),
        P("dp", "seq"),
        P(None, "dp", "seq"),
        P(None, "dp", "seq"),
    )
    out_specs = (
        P("dp", "seq"),
        P("dp", "seq"),
        P("dp", "seq"),
        P(None, "dp", "seq"),
        P(None, "dp", "seq"),
        P(None, "dp", "seq"),
    )
    return jax.shard_map(
        on_device, mesh=mesh, in_specs=in_specs, out_specs=out_specs, check_vma=False
    )
```

profile of v0, /device:TPU:4, one launch (start us, length us, event | category | flops | bytes accessed | tf_op | source)
XLA Modules:
  0.0 487.5 jit_solution(5970138415113652176)
XLA Ops:
  9.7 10.2 %all-to-all-start = ((bf16[128,32,128]{2,0,1:T(8,128)(2,1)}), bf16[128,32,128]{2,0,1:T(8,128)(2,1)S(1)}, u32[]{:S(2)}, u32[]{:S(2)}) async-start(bf16[128,32,128]{2,0,1:T(8,128)(2,1)} %bitcast.169), calls=%async_computation | async-start | bytes 2097152 | tf_op jit(solution)/shard_map/all_to_all | solution.py:163
  19.9 2.3 copy.52
  22.2 2.3 copy.53
  24.5 23.1 %all-to-all-done = bf16[128,32,128]{2,0,1:T(8,128)(2,1)S(1)} async-done(((bf16[128,32,128]{2,0,1:T(8,128)(2,1)}), bf16[128,32,128]{2,0,1:T(8,128)(2,1)S(1)}, u32[]{:S(2)}, u32[]{:S(2)}) %all-to-all-start) | async-done | bytes 1048608 | tf_op jit(solution)/shard_map/all_to_all | solution.py:163
  47.6 6.8 %all-to-all-start.1 = ((bf16[128,32,128]{2,0,1:T(8,128)(2,1)}), bf16[128,32,128]{2,0,1:T(8,128)(2,1)}, u32[]{:S(2)}, u32[]{:S(2)}) async-start(bf16[128,32,128]{2,0,1:T(8,128)(2,1)} %copy.53), calls=%async_computation.1 | async-start | bytes 2097152 | tf_op jit(solution)/shard_map/all_to_all | solution.py:161
  54.5 27.6 %all-to-all-done.1 = bf16[128,32,128]{2,0,1:T(8,128)(2,1)} async-done(((bf16[128,32,128]{2,0,1:T(8,128)(2,1)}), bf16[128,32,128]{2,0,1:T(8,128)(2,1)}, u32[]{:S(2)}, u32[]{:S(2)}) %all-to-all-start.1) | async-done | bytes 1048608 | tf_op jit(solution)/shard_map/all_to_all | solution.py:161
  83.3 6.4 %all-to-all-start.2 = ((bf16[128,32,128]{2,0,1:T(8,128)(2,1)}), bf16[128,32,128]{2,0,1:T(8,128)(2,1)}, u32[]{:S(2)}, u32[]{:S(2)}) async-start(bf16[128,32,128]{2,0,1:T(8,128)(2,1)} %bitcast.168), calls=%async_computation.2 | async-start | bytes 2097152 | tf_op jit(solution)/shard_map/all_to_all | solution.py:164
  90.5 2.3 copy.55
  92.7 2.3 copy.56
  95.1 50.0 %all-gather = s32[1,4096]{1,0:T(1,128)S(1)} all-gather(s32[1,128]{1,0:T(1,128)S(1)} %copy-done.43), channel_id=2, replica_groups=mesh['seq'=32,'dp'=16] {'seq'}, dimensions={1}, use_global_device_ids=true | all-gather | bytes 16896 | tf_op jit(solution)/shard_map/all_gather | solution.py:151
  145.1 11.3 %all-to-all-start.3 = ((bf16[128,32,128]{2,0,1:T(8,128)(2,1)}), bf16[128,32,128]{2,0,1:T(8,128)(2,1)}, u32[]{:S(2)}, u32[]{:S(2)}) async-start(bf16[128,32,128]{2,0,1:T(8,128)(2,1)} %copy.56), calls=%async_computation.3 | async-start | bytes 2097152 | tf_op jit(solution)/shard_map/all_to_all | solution.py:162
  158.6 3.2 fusion.17
  168.5 22.8 %all-to-all-done.3 = bf16[128,32,128]{2,0,1:T(8,128)(2,1)} async-done(((bf16[128,32,128]{2,0,1:T(8,128)(2,1)}), bf16[128,32,128]{2,0,1:T(8,128)(2,1)}, u32[]{:S(2)}, u32[]{:S(2)}) %all-to-all-start.3) | async-done | bytes 1048608 | tf_op jit(solution)/shard_map/all_to_all | solution.py:162
  241.1 2.0 copy-done.2
  244.6 2.4 convolution_dynamic-update-slice_fusion.7
  247.0 2.4 convolution_dynamic-update-slice_fusion.6
  249.4 3.5 fusion.110
  253.2 2.3 convolution_dynamic-update-slice_fusion.5
  255.5 2.4 convolution_dynamic-update-slice_fusion.4
  257.9 2.3 convolution_dynamic-update-slice_fusion.3
  260.2 2.4 convolution_dynamic-update-slice_fusion.2
  262.6 2.3 convolution_dynamic-update-slice_fusion.1
  264.9 2.3 convolution_dynamic-update-slice_fusion
  267.2 1.9 slice.427
  277.3 1.8 copy-done.4
  280.4 36.4 %all-gather.6.cloned.1.call-done = bf16[4096,256]{1,0:T(8,128)(2,1)} async-done(((bf16[128,256]{1,0:T(8,128)(2,1)}), bf16[4096,256]{1,0:T(8,128)(2,1)}) %all-gather.6.cloned.1.call-update) | async-done | bytes 2097168 | tf_op jit(solution)/shard_map/all_gather | solution.py:173
  316.8 3.5 fusion.10
  321.1 3.0 collective-permute-start
  324.1 7.4 %collective-permute-done = f32[2,256,64]{2,1,0:T(8,128)S(1)} collective-permute-done((f32[2,256,64]{2,1,0:T(8,128)S(1)}, f32[2,256,64]{2,1,0:T(8,128)S(1)}, u32[]{:S(2)}, u32[]{:S(2)}) %collective-permute-start) | collective-permute-done | bytes 131104 | tf_op jit(solution)/shard_map/ppermute | solution.py:20
  331.8 1.9 collective-permute-start.1
  336.1 70.0 %reduce-scatter.3.cloned.1.call-done = f32[16,128]{1,0:T(8,128)} async-done(((f32[256,128]{1,0:T(8,128)}), f32[16,128]{1,0:T(8,128)}) %reduce-scatter.3.cloned.1.call-update) | async-done | bytes 8208 | tf_op jit(solution)/shard_map/reduce_scatter | solution.py:202
  407.4 72.2 %reduce-scatter.5.cloned.1.call-done = f32[2,16,32]{2,1,0:T(8,128)} async-done(((f32[2,256,32]{2,1,0:T(8,128)}), f32[2,16,32]{2,1,0:T(8,128)}) %reduce-scatter.5.cloned.1.call-update) | async-done | bytes 4112 | tf_op jit(solution)/shard_map/reduce_scatter | solution.py:203
  (170 shorter events, 80.0 us)
Async XLA Ops:
  7.2 242.2 %copy-start = (bf16[1,128,8192]{2,1,0:T(8,128)(2,1)S(1)}, bf16[1,128,8192]{2,1,0:T(8,128)(2,1)}, u32[]{:S(2)}) copy-start(bf16[1,128,8192]{2,1,0:T(8,128)(2,1)} %param.11) | copy-start | bytes 6291460
  9.7 37.9 %all-to-all-start = ((bf16[128,32,128]{2,0,1:T(8,128)(2,1)}), bf16[128,32,128]{2,0,1:T(8,128)(2,1)S(1)}, u32[]{:S(2)}, u32[]{:S(2)}) async-start(bf16[128,32,128]{2,0,1:T(8,128)(2,1)} %bitcast.169), calls=%async_computation | async-start | bytes 2097152 | tf_op jit(solution)/shard_map/all_to_all | solution.py:163
  22.2 32.2 %copy-start.38 = (bf16[1,128,1024]{2,1,0:T(8,128)(2,1)S(1)}, bf16[1,128,1024]{2,1,0:T(8,128)(2,1)}, u32[]{:S(2)}) copy-start(bf16[1,128,1024]{2,1,0:T(8,128)(2,1)} %param.14) | copy-start | bytes 786436
  47.6 34.5 %all-to-all-start.1 = ((bf16[128,32,128]{2,0,1:T(8,128)(2,1)}), bf16[128,32,128]{2,0,1:T(8,128)(2,1)}, u32[]{:S(2)}, u32[]{:S(2)}) async-start(bf16[128,32,128]{2,0,1:T(8,128)(2,1)} %copy.53), calls=%async_computation.1 | async-start | bytes 2097152 | tf_op jit(solution)/shard_map/all_to_all | solution.py:161
  83.3 61.8 %all-to-all-start.2 = ((bf16[128,32,128]{2,0,1:T(8,128)(2,1)}), bf16[128,32,128]{2,0,1:T(8,128)(2,1)}, u32[]{:S(2)}, u32[]{:S(2)}) async-start(bf16[128,32,128]{2,0,1:T(8,128)(2,1)} %bitcast.168), calls=%async_computation.2 | async-start | bytes 2097152 | tf_op jit(solution)/shard_map/all_to_all | solution.py:164
  89.7 159.7 %all-gather.4.cloned.1.call-start = ((), (), s32[]{:S(2)}) async-start(), calls=%async_computation.6 | async-start | bytes 4456448 | tf_op jit(solution)/shard_map/all_gather | solution.py:148
  90.4 4.6 copy-start.43
  145.1 46.2 %all-to-all-start.3 = ((bf16[128,32,128]{2,0,1:T(8,128)(2,1)}), bf16[128,32,128]{2,0,1:T(8,128)(2,1)}, u32[]{:S(2)}, u32[]{:S(2)}) async-start(bf16[128,32,128]{2,0,1:T(8,128)(2,1)} %copy.56), calls=%async_computation.3 | async-start | bytes 2097152 | tf_op jit(solution)/shard_map/all_to_all | solution.py:162
  156.5 160.3 %all-gather.6.cloned.1.call-start = ((), (), s32[]{:S(2)}) async-start(), calls=%async_computation.7 | async-start | bytes 2162688 | tf_op jit(solution)/shard_map/all_gather | solution.py:173
  156.8 7.4 %copy-start.5 = (bf16[31,128,128]{2,1,0:T(8,128)(2,1)}, bf16[31,128,128]{2,1,0:T(8,128)(2,1)S(1)}, u32[]{:S(2)}) copy-start(bf16[31,128,128]{2,1,0:T(8,128)(2,1)S(1)} %slice.376) | copy-start | bytes 3047428
  158.5 4.3 copy-start.7
  162.9 2.7 copy-start.10
  220.1 2.7 copy-start.8
  220.1 2.7 copy-start.18
  224.1 2.5 copy-start.24
  225.4 2.5 copy-start.19
  231.8 2.5 copy-start.30
  252.9 153.1 %reduce-scatter.3.cloned.1.call-start = ((), (), s32[]{:S(2)}) async-start(), calls=%async_computation.8 | async-start | bytes 139264 | tf_op jit(solution)/shard_map/reduce_scatter | solution.py:202
  269.1 3.1 copy-start.29
  269.1 7.7 %copy-start.3 = (f32[32,256,128]{2,1,0:T(8,128)S(1)}, f32[32,256,128]{2,1,0:T(8,128)}, u32[]{:S(2)}) copy-start(f32[32,256,128]{2,1,0:T(8,128)} %copy-done.2) | copy-start | bytes 12582916
  269.4 3.8 copy-start.31
  269.4 4.7 copy-start.33
  269.4 5.6 %copy-start.35 = (bf16[4,128,256]{1,2,0:T(8,128)(2,1)S(1)}, bf16[4,128,256]{1,2,0:T(8,128)(2,1)}, u32[]{:S(2)}) copy-start(bf16[4,128,256]{1,2,0:T(8,128)(2,1)} %copy-done.34) | copy-start | bytes 786436
  270.3 5.6 %copy-start.37 = (bf16[4,128,256]{1,2,0:T(8,128)(2,1)S(1)}, bf16[4,128,256]{1,2,0:T(8,128)(2,1)}, u32[]{:S(2)}) copy-start(bf16[4,128,256]{1,2,0:T(8,128)(2,1)} %copy-done.36) | copy-start | bytes 786436
  271.3 5.6 %copy-start.1 = (f32[31,128,128]{2,1,0:T(8,128)S(1)}, f32[31,128,128]{2,1,0:T(8,128)}, u32[]{:S(2)}) copy-start(f32[31,128,128]{2,1,0:T(8,128)} %slice.425) | copy-start | bytes 6094852
  320.3 85.8 %copy-start.41 = (f32[16,128]{1,0:T(8,128)S(1)}, f32[16,128]{1,0:T(8,128)}, u32[]{:S(2)}) copy-start(f32[16,128]{1,0:T(8,128)} %param.19) | copy-start | bytes 24580
  320.3 85.8 %copy-start.42 = (f32[16,128]{1,0:T(8,128)S(1)}, f32[16,128]{1,0:T(8,128)}, u32[]{:S(2)}) copy-start(f32[16,128]{1,0:T(8,128)} %param.18) | copy-start | bytes 24580
  320.3 159.3 %copy-start.39 = (f32[2,16,32]{2,1,0:T(8,128)S(1)}, f32[2,16,32]{2,1,0:T(8,128)}, u32[]{:S(2)}) copy-start(f32[2,16,32]{2,1,0:T(8,128)} %param.21) | copy-start | bytes 12292
  320.3 159.3 %copy-start.40 = (f32[2,16,32]{2,1,0:T(8,128)S(1)}, f32[2,16,32]{2,1,0:T(8,128)}, u32[]{:S(2)}) copy-start(f32[2,16,32]{2,1,0:T(8,128)} %param.20) | copy-start | bytes 12292
  321.1 10.3 %collective-permute-start = (f32[2,256,64]{2,1,0:T(8,128)S(1)}, f32[2,256,64]{2,1,0:T(8,128)S(1)}, u32[]{:S(2)}, u32[]{:S(2)}) collective-permute-start(f32[2,256,64]{2,1,0:T(8,128)S(1)} %fusion.129), channel_id=1, source_target_pairs={{0,32},{16,48},{32,0},{48,16},{64,96},{80,112},{96,64},{112,80},{1... | collective-permute-start | bytes 393224 | tf_op jit(solution)/shard_map/ppermute | solution.py:20
  331.8 3.4 collective-permute-start.1
  333.7 145.9 %reduce-scatter.5.cloned.1.call-start = ((), (), s32[]{:S(2)}) async-start(), calls=%async_computation.9 | async-start | bytes 278528 | tf_op jit(solution)/shard_map/reduce_scatter | solution.py:203
  (22 other events, 41.2 us)
Sparse Core Ops, SparseCore 0:
  92.6 139.3 all-gather.3
  253.0 63.7 all-gather.5
  333.8 72.1 reduce-scatter.2
  408.9 70.6 reduce-scatter.4
where the time goes:
time: 489 us; the launch traced here: 487 us
  waiting for transfers between devices  262 us (54%)
  matrix products  77.1 us (16%)
  blocking collectives  50 us (10%)
  starting transfers between devices  40.2 us (8%)
  local copies, waits for them, and re-layouts  27.3 us (6%)
  other arithmetic  16.6 us (3%)
  between operations  14.6 us (3%)
    reduce_scatter x1, waiting for transfers between devices, on_device(): lax.psum_scatter(block_cols, 'dp', scatter_dimension=1, tiled=True)  72.2 us
    reduce_scatter x1, waiting for transfers between devices, on_device(): lax.psum_scatter(query_terms, 'dp', scatter_dimension=0, tiled=True)  70 us
    all_gather x1, blocking collectives, on_device(): documents = lax.all_gather(doc_ids[0], 'seq', axis=0, tiled=True)  50 us
    all_gather x1, waiting for transfers between devices, on_device(): lax.all_gather(lowrank, 'seq', axis=0, tiled=True)  36.4 us
    all_to_all x1, waiting for transfers between devices, on_device(): lax.all_to_all(query_rows, 'seq', split_axis=1, concat_axis=0, tiled=True)  27.6 us
    all_to_all x1, waiting for transfers between devices, on_device(): lax.all_to_all(key_rows, 'seq', split_axis=1, concat_axis=0, tiled=True)  23.1 us
    all_to_all x1, waiting for transfers between devices, on_device(): lax.all_to_all(grad_rows, 'seq', split_axis=1, concat_axis=0, tiled=True)  22.8 us
    dot_general x8, matrix products, head_grads(): jnp.einsum('sqk,sqd->skd', attention_low, grad_block, preferred_element_t...  18.8 us
  transfers between devices with their start and end apart: 10, of which 8 were waited for; matrix products, arithmetic and copies ran while one was open for 20% of the time, Pallas kernels for 0%

commit v1 on v0

v1 whole, which is shorter than its diff:
```python
import jax
import jax.numpy as jnp
from jax import lax
from jax.experimental import pallas as pl
from jax.experimental.pallas import tpu as pltpu
from jax.sharding import PartitionSpec as P

H = 32
KVH = 8
HD = 128
RANK = 256
TOK = 128
DEPTH = 8192
ADAM_STEP = 100

beta_first = 0.9
beta_second = 0.999
adam_epsilon = 1e-08

MESH = pl.DeviceIdType.MESH
SIZES = {"core": 2, "x": 4, "y": 8, "z": 8}
BF = jnp.bfloat16
F32 = jnp.float32
QCOLS = H * HD
KCOLS = KVH * HD
PIECES = 4
PIECE = KCOLS // PIECES
BLOCK = 512
HALF = 256
QUARTER = 128


def rem(a, n):
    return lax.rem(a, n)


def here():
    s = lax.axis_index("seq")
    d = lax.axis_index("dp")
    return {
        "core": rem(s, 2),
        "x": rem(s // 2, 4),
        "y": (s // 8) * 2 + rem(d, 2),
        "z": d // 2,
    }


def device(c):
    return {
        "seq": (c["y"] // 2) * 8 + c["x"] * 2 + c["core"],
        "dp": c["z"] * 2 + rem(c["y"], 2),
    }


def moved(c, axis, k):
    n = SIZES[axis]
    out = dict(c)
    out[axis] = rem(c[axis] + (k % n), n)
    return out


def dot_rows(a, b):
    return lax.dot_general(a, b, (((1,), (1,)), ((), ())), preferred_element_type=F32)


def dot_plain(a, b):
    return lax.dot_general(a, b, (((1,), (0,)), ((), ())), preferred_element_type=F32)


def dot_first(a, b):
    return lax.dot_general(a, b, (((0,), (0,)), ((), ())), preferred_element_type=F32)


def kernel(
    hid_in, q_in, k_in, v_in, g_in, doc_in, proj_in,
    outq_ref, outkv_ref,
    hid, q, g, kw, vw, docs, bias, pg, dq, dk, dv, lr, dup, perm,
    zq, rq, xq, xr, yq, yr, wq, wr,
    zk, rk, ck, cr, xk, xkr, yk, ykr, kv_sum,
    load_sem,
    halo_send, halo_recv,
    gz_send, gz_recv, gy_send, gy_recv, gc_send, gc_recv,
    rc_send, rc_recv, qx_send, qx_recv, qy_send, qy_recv, qz_send, qz_recv,
    kz_send, kz_recv, kx_send, kx_recv, ky_send, ky_recv,
):
    c = here()
    s = lax.axis_index("seq")
    d = lax.axis_index("dp")
    core, x, y, z = c["core"], c["x"], c["y"], c["z"]
    y_lo = rem(y, 2)
    nxt = {"seq": rem(s + 1, 32), "dp": d}
    prv = {"seq": rem(s + 31, 32), "dp": d}
    sibling = device(moved(c, "core", 1))

    def zstep(k):
        return rem(z + jnp.where(core == 0, k + 8, 8 - k), 8)

    def zdev(k):
        n = dict(c)
        n["z"] = zstep(k)
        return device(n)

    barrier = pltpu.get_barrier_semaphore()
    peers = [nxt, prv, sibling]
    for axis in ("x", "y", "z"):
        for k in range(1, SIZES[axis]):
            peers.append(device(moved(c, axis, k)))
    for p in peers:
        pl.semaphore_signal(barrier, inc=1, device_id=p, device_id_type=MESH)

    loads = [
        pltpu.make_async_copy(doc_in, docs.at[0], load_sem.at[0]),
        pltpu.make_async_copy(k_in, kw.at[pl.ds(TOK, TOK)], load_sem.at[1]),
        pltpu.make_async_copy(v_in, vw.at[pl.ds(TOK, TOK)], load_sem.at[2]),
        pltpu.make_async_copy(q_in, q, load_sem.at[3]),
        pltpu.make_async_copy(g_in, g, load_sem.at[4]),
        pltpu.make_async_copy(
            proj_in, pg.at[pl.ds(pl.multiple_of(d * BLOCK, BLOCK), BLOCK)], load_sem.at[5]
        ),
        pltpu.make_async_copy(hid_in, hid, load_sem.at[6]),
    ]
    for cp in loads:
        cp.start()

    pl.semaphore_wait(barrier, len(peers))

    def remote(src, dst, send, recv, to):
        return pltpu.make_async_remote_copy(
            src_ref=src, dst_ref=dst, send_sem=send, recv_sem=recv, device_id=to, device_id_type=MESH
        )

    sent = []

    def go(cp):
        cp.start()
        sent.append(cp)
        return cp

    def prow(w, b, h, u=None):
        if u is None:
            return pg.at[pl.ds(pl.multiple_of((w * 2 + b) * BLOCK + h * HALF, HALF), HALF)]
        return pg.at[pl.ds(pl.multiple_of((w * 2 + b) * BLOCK + h * HALF + u * QUARTER, QUARTER), QUARTER)]

    own_half = proj_in.at[pl.ds(pl.multiple_of(core * HALF, HALF), HALF)]

    def own_quarter(u):
        return proj_in.at[pl.ds(pl.multiple_of(core * HALF + u * QUARTER, QUARTER), QUARTER)]

    zf, zb = zdev(1), zdev(-1)
    yu, yd = device(moved(c, "y", 1)), device(moved(c, "y", -1))
    go(remote(own_half, prow(z, y_lo, core), gz_send.at[0], gz_recv.at[0], zf))
    go(remote(own_half, prow(z, y_lo, core), gz_send.at[4], gz_recv.at[4], zb))
    halo = []
    for i in range(PIECES):
        cols = pl.ds(i * PIECE, PIECE)
        a = remote(k_in.at[:, cols], kw.at[pl.ds(0, TOK), cols], halo_send.at[i], halo_recv.at[i], nxt)
        b = remote(
            v_in.at[:, cols], vw.at[pl.ds(0, TOK), cols], halo_send.at[PIECES + i], halo_recv.at[PIECES + i], nxt
        )
        if i == 0:
            loads[0].wait()
            go(remote(docs.at[0], docs.at[1], halo_send.at[2 * PIECES], halo_recv.at[2 * PIECES], nxt))
        go(a)
        go(b)
        halo.append((a, b))

    def y_sends(slot, srcs, w):
        go(remote(srcs[0], prow(w, y_lo, core, 0), gy_send.at[2 * slot], gy_recv.at[2 * slot], yu))
        go(remote(srcs[1], prow(w, y_lo, core, 1), gy_send.at[2 * slot + 1], gy_recv.at[2 * slot + 1], yd))

    y_sends(0, [own_quarter(0), own_quarter(1)], z)

    def core_send(slot, w, b):
        ref = prow(w, b, core)
        go(remote(ref, ref, gc_send.at[slot], gc_recv.at[slot], sibling))

    def z_arrival(slot, k):
        w = zstep(-k)
        ref = prow(w, y_lo, core)
        last = slot in (3, 6)
        remote(ref, ref, gz_send.at[slot], gz_recv.at[slot], zf).wait_recv()
        if not last:
            go(remote(ref, ref, gz_send.at[slot + 1], gz_recv.at[slot + 1], zf if slot < 4 else zb))
        y_sends(slot + 1, [prow(w, y_lo, core, 0), prow(w, y_lo, core, 1)], w)
        core_send(slot, w, y_lo)

    def y_arrival(slot, k):
        w = zstep(-k)
        for u, frm in ((0, yu), (1, yd)):
            ref = prow(w, 1 - y_lo, core, u)
            remote(ref, ref, gy_send.at[2 * slot + u], gy_recv.at[2 * slot + u], frm).wait_recv()
        core_send(7 + slot, w, 1 - y_lo)

    def core_arrival(slot, k, b):
        ref = prow(zstep(k), b, 1 - core)
        remote(ref, ref, gc_send.at[slot], gc_recv.at[slot], sibling).wait_recv()

    z_order = [(0, 1), (4, -1), (1, 2), (5, -2), (2, 3), (6, -3), (3, 4)]
    y_order = [(0, 0)] + [(slot + 1, k) for slot, k in z_order]

    remote(docs.at[0], docs.at[1], halo_send.at[2 * PIECES], halo_recv.at[2 * PIECES], nxt).wait_recv()
    mine = jnp.broadcast_to(docs[0].astype(F32), (TOK, TOK))
    before = jnp.broadcast_to(docs[1].astype(F32), (TOK, TOK))
    before = jnp.where(s == 0, -1.0, before)
    rows = jnp.transpose(mine)
    causal = lax.broadcasted_iota(jnp.int32, (TOK, TOK), 1) <= lax.broadcasted_iota(jnp.int32, (TOK, TOK), 0)
    bias[:, TOK:] = jnp.where(causal & (mine == rows), 0.0, -jnp.inf)
    bias[:, :TOK] = jnp.where(before == rows, 0.0, -jnp.inf)

    ri = lax.broadcasted_iota(jnp.int32, (RANK, 512), 0)
    ci = lax.broadcasted_iota(jnp.int32, (RANK, 512), 1)
    want = ((ci & 127) >> 3) * 16 + (ci >> 7) * 4 + (ci & 3)
    dup[...] = jnp.where(ri == want, 1.0, 0.0).astype(BF)
    ri = lax.broadcasted_iota(jnp.int32, (512, 512), 0)
    ci = lax.broadcasted_iota(jnp.int32, (512, 512), 1)
    want = ((ci & 127) >> 5) * 128 + (ci >> 7) * 32 + (ci & 31)
    perm[...] = jnp.where(ri == want, 1.0, 0.0).astype(BF)

    score_scale = 1.0 / HD**0.5

    def attend(gi, carry):
        wide = pl.multiple_of(gi * 512, 512)
        thin = pl.multiple_of(gi * HD, HD)
        qh = [q[:, pl.ds(wide + j * HD, HD)] for j in range(4)]
        gh = [g[:, pl.ds(wide + j * HD, HD)] for j in range(4)]
        q4 = jnp.concatenate(qh, axis=0)
        g4 = jnp.concatenate(gh, axis=0)
        kwin = kw[:, pl.ds(thin, HD)]
        vwin = vw[:, pl.ds(thin, HD)]
        sc = dot_rows(q4, kwin).reshape(4, TOK, 256) * score_scale + bias[...][None]
        sc = sc.reshape(512, 256)
        peak = jnp.max(sc, axis=1, keepdims=True)
        e = jnp.exp(sc - peak)
        att = e * (1.0 / jnp.sum(e, axis=1, keepdims=True))
        low = att.astype(BF)
        da = dot_rows(g4, vwin)
        delta = jnp.sum(low.astype(F32) * da, axis=1, keepdims=True)
        ds = (att * (da - delta)).astype(BF)
        dqv = (dot_plain(ds, kwin) * score_scale).astype(BF)
        for j in range(4):
            dq[:, pl.ds(wide + j * HD, HD)] = dqv[j * TOK : (j + 1) * TOK]
        dk[:, pl.ds(thin, HD)] = (dot_first(ds, q4) * score_scale).astype(BF)
        dv[:, pl.ds(thin, HD)] = dot_first(low, g4).astype(BF)
        return carry

    def halo_wait(i):
        for cp in halo[i]:
            cp.wait_recv()

    for cp in loads[1:5]:
        cp.wait()
    halo_wait(0)
    lax.fori_loop(0, 2, attend, 0)
    z_arrival(*z_order[0])
    z_arrival(*z_order[1])
    y_arrival(*y_order[0])
    halo_wait(1)
    lax.fori_loop(2, 4, attend, 0)
    z_arrival(*z_order[2])
    z_arrival(*z_order[3])
    y_arrival(*y_order[1])
    y_arrival(*y_order[2])
    halo_wait(2)
    lax.fori_loop(4, 6, attend, 0)
    z_arrival(*z_order[4])
    z_arrival(*z_order[5])
    y_arrival(*y_order[3])
    y_arrival(*y_order[4])
    halo_wait(3)
    lax.fori_loop(6, 8, attend, 0)
    z_arrival(*z_order[6])
    for i in range(5, 8):
        y_arrival(*y_order[i])
    for slot, k in z_order:
        core_arrival(slot, k, y_lo)
    for slot, k in y_order:
        core_arrival(7 + slot, k, 1 - y_lo)
    loads[5].wait()
    loads[6].wait()

    lr[pl.ds(TOK, TOK)] = dot_plain(hid[...], pg[...]).astype(BF)
    lr_copy = go(
        remote(lr.at[pl.ds(TOK, TOK)], lr.at[pl.ds(0, TOK)], halo_send.at[2 * PIECES + 1], halo_recv.at[2 * PIECES + 1], nxt)
    )
    own_lr = lr[pl.ds(TOK, TOK)]

    def project(gi):
        part = dot_first(own_lr, dq[:, pl.ds(pl.multiple_of(gi * 512, 512), 512)]).astype(BF)
        for j in range(4):
            piece = part[:, j * HD : (j + 1) * HD].reshape(8, 2, 16, HD)
            at_x = rem(2 * gi + j // 2, 4)
            for lo in range(2):
                zq[j % 2, at_x, (gi // 2) * 2 + lo] = piece[:, lo]

    def project_even(i, carry):
        project(2 * i)
        return carry

    def project_odd(i, carry):
        project(2 * i + 1)
        return carry

    lax.fori_loop(0, 4, project_even, 0)
    qc = [go(remote(zq.at[1 - core, pl.ds(0, 2)], rq.at[pl.ds(0, 2)], rc_send.at[0], rc_recv.at[0], sibling))]
    lax.fori_loop(0, 4, project_odd, 0)
    qc.append(go(remote(zq.at[1 - core, pl.ds(2, 2)], rq.at[pl.ds(2, 2)], rc_send.at[1], rc_recv.at[1], sibling)))

    lr_copy.wait_recv()
    spread = dot_plain(lr[...], dup[...]).astype(BF)
    kind = (lax.broadcasted_iota(jnp.int32, (256, 512), 1) >> 2) & 1
    left_k = jnp.where(kind == 0, spread, jnp.zeros_like(spread))
    left_v = jnp.where(kind == 1, spread, jnp.zeros_like(spread))
    for a in range(KVH):
        cols = slice(a * HD, (a + 1) * HD)
        both = (dot_first(left_k, dk[:, cols]) + dot_first(left_v, dv[:, cols])).astype(BF)
        wide = jnp.concatenate([both[i * 128 : (i + 1) * 128] for i in range(4)], axis=1)
        wide = dot_plain(wide, perm[...]).astype(BF)
        for b in range(4):
            zk[b % 2, :, (a % 2) * 2 + b // 2, a // 2] = wide[:, b * HD : (b + 1) * HD].reshape(8, 16, HD)
    kc = go(remote(zk.at[1 - core], rk, rc_send.at[2], rc_recv.at[2], sibling))

    for cp in qc:
        cp.wait_recv()
    qx = []
    for k in (2, 1, 3, 0):
        at = rem(x + k, 4)
        xq[at] = (zq[core, at].astype(F32) + rq[at].astype(F32)).astype(BF)
        if k:
            qx.append(go(remote(xq.at[at], xr.at[k - 1], qx_send.at[k - 1], qx_recv.at[k - 1], device(moved(c, "x", k)))))
    kc.wait_recv()
    kz = []
    for k in (4, 3, 5, 2, 6, 1, 7, 0):
        at = rem(z + k, 8)
        ck[at] = (zk[core, at].astype(F32) + rk[at].astype(F32)).astype(BF)
        if k:
            kz.append(go(remote(ck.at[at], cr.at[k - 1], kz_send.at[k - 1], kz_recv.at[k - 1], device(moved(c, "z", k)))))

    for cp in qx:
        cp.wait_recv()
    qy = []
    for k in (4, 3, 5, 2, 6, 1, 7, 0):
        at = rem(y + k, 8)
        tot = xq[x, at].astype(F32)
        for i in range(3):
            tot = tot + xr[i, at].astype(F32)
        yq[at] = tot.astype(BF)
        if k:
            qy.append(go(remote(yq.at[at], yr.at[k - 1], qy_send.at[k - 1], qy_recv.at[k - 1], device(moved(c, "y", k)))))
    for cp in kz:
        cp.wait_recv()
    kx = []
    for k in (2, 1, 3, 0):
        at = rem(x + k, 4)
        tot = ck[z, at].astype(F32)
        for i in range(7):
            tot = tot + cr[i, at].astype(F32)
        xk[at] = tot.astype(BF)
        if k:
            kx.append(go(remote(xk.at[at], xkr.at[k - 1], kx_send.at[k - 1], kx_recv.at[k - 1], device(moved(c, "x", k)))))
    for cp in qy:
        cp.wait_recv()
    tot = yq[y].astype(F32)
    for i in range(7):
        tot = tot + yr[i].astype(F32)
    wq[...] = tot.astype(BF)
    qz = []
    for k in (4, 3, 5, 2, 6, 1, 7):
        at = rem(z + k, 8)
        qz.append(go(remote(wq.at[at], wr.at[k - 1], qz_send.at[k - 1], qz_recv.at[k - 1], device(moved(c, "z", k)))))
    for cp in kx:
        cp.wait_recv()
    tot = xk[x].astype(F32)
    for i in range(3):
        tot = tot + xkr[i].astype(F32)
    yk[...] = tot.astype(BF)
    ky = []
    for k in (4, 3, 5, 2, 6, 1, 7):
        to = moved(c, "y", k)
        ky.append(go(remote(yk.at[to["y"] // 2], ykr.at[k - 1], ky_send.at[k - 1], ky_recv.at[k - 1], device(to))))
    for cp in qz:
        cp.wait_recv()
    tot = wq[z].astype(F32)
    for i in range(7):
        tot = tot + wr[i].astype(F32)
    outq_ref[...] = tot
    for cp in ky:
        cp.wait_recv()
    tot = yk[y // 2].astype(F32)
    for i in range(7):
        tot = tot + ykr[i].astype(F32)
    kv_sum[...] = tot
    outkv_ref[...] = kv_sum[pl.ds(pl.multiple_of(y_lo * 8, 8), 8)]
    for cp in sent:
        cp.wait_send()


def reduced(hid, q, k, v, g, docs, proj):
    any_spec = pl.BlockSpec(memory_space=pl.ANY)
    vmem = pl.BlockSpec(memory_space=pltpu.VMEM)
    dma = pltpu.SemaphoreType.DMA
    halos = 2 * PIECES + 2
    scratch = [
        pltpu.VMEM((TOK, DEPTH), BF),
        pltpu.VMEM((TOK, QCOLS), BF),
        pltpu.VMEM((TOK, QCOLS), BF),
        pltpu.VMEM((2 * TOK, KCOLS), BF),
        pltpu.VMEM((2 * TOK, KCOLS), BF),
        pltpu.VMEM((2, 1, TOK), jnp.int32),
        pltpu.VMEM((TOK, 2 * TOK), F32),
        pltpu.VMEM((DEPTH, RANK), BF),
        pltpu.VMEM((TOK, QCOLS), BF),
        pltpu.VMEM((2 * TOK, KCOLS), BF),
        pltpu.VMEM((2 * TOK, KCOLS), BF),
        pltpu.VMEM((2 * TOK, RANK), BF),
        pltpu.VMEM((RANK, 512), BF),
        pltpu.VMEM((512, 512), BF),
        pltpu.VMEM((2, 4, 8, 8, 16, HD), BF),
        pltpu.VMEM((4, 8, 8, 16, HD), BF),
        pltpu.VMEM((4, 8, 8, 16, HD), BF),
        pltpu.VMEM((3, 8, 8, 16, HD), BF),
        pltpu.VMEM((8, 8, 16, HD), BF),
        pltpu.VMEM((7, 8, 16, HD), BF),
        pltpu.VMEM((8, 16, HD), BF),
        pltpu.VMEM((7, 16, HD), BF),
        pltpu.VMEM((2, 8, 4, 4, 16, HD), BF),
        pltpu.VMEM((8, 4, 4, 16, HD), BF),
        pltpu.VMEM((8, 4, 4, 16, HD), BF),
        pltpu.VMEM((7, 4, 4, 16, HD), BF),
        pltpu.VMEM((4, 4, 16, HD), BF),
        pltpu.VMEM((3, 4, 16, HD), BF),
        pltpu.VMEM((4, 16, HD), BF),
        pltpu.VMEM((7, 16, HD), BF),
        pltpu.VMEM((16, HD), F32),
        dma((7,)),
    ]
    for n in (halos, 7, 16, 15, 3, 3, 7, 7, 7, 3, 7):
        scratch += [dma((n,)), dma((n,))]
    return pl.pallas_call(
        kernel,
        out_shape=(jax.ShapeDtypeStruct((16, HD), F32), jax.ShapeDtypeStruct((8, HD), F32)),
        in_specs=[any_spec] * 7,
        out_specs=(vmem, vmem),
        scratch_shapes=scratch,
        compiler_params=pltpu.CompilerParams(
            collective_id=0, has_side_effects=True, vmem_limit_bytes=48 * 1024 * 1024
        ),
        name="backward",
    )(hid, q, k, v, g, docs, proj)


def adam_update(first_moment, second_moment, gradient):
    first_new = beta_first * first_moment + (1.0 - beta_first) * gradient
    second_new = beta_second * second_moment + (1.0 - beta_second) * gradient * gradient
    corrected_first = first_new / (1.0 - beta_first**ADAM_STEP)
    corrected_second = second_new / (1.0 - beta_second**ADAM_STEP)
    return (first_new, second_new, corrected_first / (jnp.sqrt(corrected_second) + adam_epsilon))


def on_device(
    hidden_in, queries, keys, values, out_grad, doc_ids, projection, mom1_q, mom2_q, mom1_kv, mom2_kv
):
    grad_q, grad_kv = reduced(
        hidden_in[0], queries[0], keys[0], values[0], out_grad[0], doc_ids, projection
    )
    grad_kv = grad_kv.reshape(2, 4, 4, 32).transpose(0, 2, 1, 3).reshape(2, 16, 32)
    return adam_update(mom1_q, mom2_q, grad_q) + adam_update(mom1_kv, mom2_kv, grad_kv)


def solution(mesh):
    in_specs = (
        P("dp", "seq", None),
        P("dp", "seq", None),
        P("dp", "seq", None),
        P("dp", "seq", None),
        P("dp", "seq", None),
        P("dp", "seq"),
        P("dp", None),
        P("dp", "seq"),
        P("dp", "seq"),
        P(None, "dp", "seq"),
        P(None, "dp", "seq"),
    )
    out_specs = (
        P("dp", "seq"),
        P("dp", "seq"),
        P("dp", "seq"),
        P(None, "dp", "seq"),
        P(None, "dp", "seq"),
        P(None, "dp", "seq"),
    )
    return jax.shard_map(
        on_device, mesh=mesh, in_specs=in_specs, out_specs=out_specs, check_vma=False
    )
```

time: 489 us -> 86.3 us (0.18)
  the two profiles are of different devices: /device:TPU:4 before, /device:TPU:2 now
where the time goes in v1:
time: 86.3 us; the launch traced here: 85.9 us
  Pallas kernels  76.4 us (89%)
  local copies, waits for them, and re-layouts  7.64 us (9%)
  other arithmetic  1.25 us (1%)
    pallas_call x1, Pallas kernels, reduced(): pl.pallas_call(kernel, out_shape=(jax.ShapeDtypeStruct((16, HD), F32), ja...  76.4 us
    unnamed x22, local copies, waits for them, and re-layouts  7.55 us

profile of v1, /device:TPU:2, one launch (start us, length us, event | category | flops | bytes accessed | tf_op | source)
XLA Modules:
  0.0 85.9 jit_solution(6025234155005605198)
XLA Ops:
  0.6 0.0 copy-start
  0.6 1.6 %copy-done = bf16[1,128,8192]{2,1,0:T(8,128)(2,1)S(1)} copy-done((bf16[1,128,8192]{2,1,0:T(8,128)(2,1)S(1)}, bf16[1,128,8192]{2,1,0:T(8,128)(2,1)}, u32[]{:S(2)}) %copy-start) | copy-done | bytes 2097176
  2.2 0.0 copy-start.1
  2.2 1.2 %copy-done.1 = bf16[1,128,4096]{2,1,0:T(8,128)(2,1)S(1)} copy-done((bf16[1,128,4096]{2,1,0:T(8,128)(2,1)S(1)}, bf16[1,128,4096]{2,1,0:T(8,128)(2,1)}, u32[]{:S(2)}) %copy-start.1) | copy-done | bytes 1048600
  3.5 0.0 copy-start.2
  3.5 1.2 %copy-done.2 = bf16[1,128,4096]{2,1,0:T(8,128)(2,1)S(1)} copy-done((bf16[1,128,4096]{2,1,0:T(8,128)(2,1)S(1)}, bf16[1,128,4096]{2,1,0:T(8,128)(2,1)}, u32[]{:S(2)}) %copy-start.2) | copy-done | bytes 1048600
  4.7 0.0 copy-start.3
  4.7 0.9 %copy-done.3 = bf16[1,128,1024]{2,1,0:T(8,128)(2,1)S(1)} copy-done((bf16[1,128,1024]{2,1,0:T(8,128)(2,1)S(1)}, bf16[1,128,1024]{2,1,0:T(8,128)(2,1)}, u32[]{:S(2)}) %copy-start.3) | copy-done | bytes 262168
  5.6 0.0 copy-start.4
  5.6 0.9 %copy-done.4 = bf16[1,128,1024]{2,1,0:T(8,128)(2,1)S(1)} copy-done((bf16[1,128,1024]{2,1,0:T(8,128)(2,1)S(1)}, bf16[1,128,1024]{2,1,0:T(8,128)(2,1)}, u32[]{:S(2)}) %copy-start.4) | copy-done | bytes 262168
  6.6 0.0 copy-start.5
  6.6 0.9 %copy-done.5 = bf16[512,256]{1,0:T(8,128)(2,1)S(1)} copy-done((bf16[512,256]{1,0:T(8,128)(2,1)S(1)}, bf16[512,256]{1,0:T(8,128)(2,1)}, u32[]{:S(2)}) %copy-start.5) | copy-done | bytes 262168
  7.5 0.0 copy-start.6
  7.5 0.7 copy-done.6
  8.2 0.0 copy-start.7
  8.2 0.0 copy-start.8
  8.2 0.0 copy-start.9
  8.2 0.0 copy-start.10
  8.2 76.4 %backward.1 = (f32[16,128]{1,0:T(8,128)S(1)}, f32[8,128]{1,0:T(8,128)S(1)}) custom-call(bf16[128,8192]{1,0:T(8,128)(2,1)S(1)} %bitcast.7, bf16[128,4096]{1,0:T(8,128)(2,1)S(1)} %bitcast.8, bf16[128,1024]{1,0:T(8,128)(2,1)S(1)} %bitcast.10, bf16[128,1024]{1,0:T(8,128)(2,1)S(1)} %bitcast.11, bf16[128,4096]{1,0:T(8,128)(2,1)S(1)} %bitcast.9, ...), custom_call_target="tpu_custom_call" | custom-call | tf_op jit(solution)/shard_map/backward/pallas_call | solution.py:438
  84.6 0.1 reshape.18
  84.7 0.0 copy-done.7
  84.7 0.0 copy-done.8
  84.7 0.6 add_divide_fusion
  85.3 0.0 copy-done.9
  85.3 0.0 copy-done.10
  85.3 0.6 add_divide_fusion.1
  (1 shorter events, 0.0 us)
Async XLA Ops:
  0.6 1.6 %copy-start = (bf16[1,128,8192]{2,1,0:T(8,128)(2,1)S(1)}, bf16[1,128,8192]{2,1,0:T(8,128)(2,1)}, u32[]{:S(2)}) copy-start(bf16[1,128,8192]{2,1,0:T(8,128)(2,1)} %param.11) | copy-start | bytes 6291460
  2.2 1.2 %copy-start.1 = (bf16[1,128,4096]{2,1,0:T(8,128)(2,1)S(1)}, bf16[1,128,4096]{2,1,0:T(8,128)(2,1)}, u32[]{:S(2)}) copy-start(bf16[1,128,4096]{2,1,0:T(8,128)(2,1)} %param.12) | copy-start | bytes 3145732
  3.5 1.2 %copy-start.2 = (bf16[1,128,4096]{2,1,0:T(8,128)(2,1)S(1)}, bf16[1,128,4096]{2,1,0:T(8,128)(2,1)}, u32[]{:S(2)}) copy-start(bf16[1,128,4096]{2,1,0:T(8,128)(2,1)} %param.15) | copy-start | bytes 3145732
  4.7 0.9 %copy-start.3 = (bf16[1,128,1024]{2,1,0:T(8,128)(2,1)S(1)}, bf16[1,128,1024]{2,1,0:T(8,128)(2,1)}, u32[]{:S(2)}) copy-start(bf16[1,128,1024]{2,1,0:T(8,128)(2,1)} %param.13) | copy-start | bytes 786436
  5.6 0.9 %copy-start.4 = (bf16[1,128,1024]{2,1,0:T(8,128)(2,1)S(1)}, bf16[1,128,1024]{2,1,0:T(8,128)(2,1)}, u32[]{:S(2)}) copy-start(bf16[1,128,1024]{2,1,0:T(8,128)(2,1)} %param.14) | copy-start | bytes 786436
  6.6 0.9 %copy-start.5 = (bf16[512,256]{1,0:T(8,128)(2,1)S(1)}, bf16[512,256]{1,0:T(8,128)(2,1)}, u32[]{:S(2)}) copy-start(bf16[512,256]{1,0:T(8,128)(2,1)} %proj_in.1) | copy-start | bytes 786436
  7.5 0.7 copy-start.6
  8.2 76.5 %copy-start.7 = (f32[2,16,32]{2,1,0:T(8,128)S(1)}, f32[2,16,32]{2,1,0:T(8,128)}, u32[]{:S(2)}) copy-start(f32[2,16,32]{2,1,0:T(8,128)} %param.21) | copy-start | bytes 12292
  8.2 76.5 %copy-start.8 = (f32[2,16,32]{2,1,0:T(8,128)S(1)}, f32[2,16,32]{2,1,0:T(8,128)}, u32[]{:S(2)}) copy-start(f32[2,16,32]{2,1,0:T(8,128)} %param.20) | copy-start | bytes 12292
  8.2 77.1 %copy-start.9 = (f32[16,128]{1,0:T(8,128)S(1)}, f32[16,128]{1,0:T(8,128)}, u32[]{:S(2)}) copy-start(f32[16,128]{1,0:T(8,128)} %param.19) | copy-start | bytes 24580
  8.2 77.1 %copy-start.10 = (f32[16,128]{1,0:T(8,128)S(1)}, f32[16,128]{1,0:T(8,128)}, u32[]{:S(2)}) copy-start(f32[16,128]{1,0:T(8,128)} %param.18) | copy-start | bytes 24580

commit v2 on v1

--- a/solution.py
+++ b/solution.py
@@ -74,10 +74,12 @@
 def kernel(
     hid_in, q_in, k_in, v_in, g_in, doc_in, proj_in,
     outq_ref, outkv_ref,
-    hid, q, g, kw, vw, docs, bias, pg, dq, dk, dv, lr, dup, perm,
+    hid, q, g, kw, vw, docs, bias, pg, dq, dkv, acc, lr, left, dup, perm,
     zq, rq, xq, xr, yq, yr, wq, wr,
     zk, rk, ck, cr, xk, xkr, yk, ykr, kv_sum,
+    relay,
     load_sem,
+    rel_send, rel_recv,
     halo_send, halo_recv,
     gz_send, gz_recv, gy_send, gy_recv, gc_send, gc_recv,
     rc_send, rc_recv, qx_send, qx_recv, qy_send, qy_recv, qz_send, qz_recv,
@@ -91,6 +93,11 @@
     nxt = {"seq": rem(s + 1, 32), "dp": d}
     prv = {"seq": rem(s + 31, 32), "dp": d}
     sibling = device(moved(c, "core", 1))
+    across = device(
+        {"core": 1 - core, "x": rem(x + jnp.where(core == 1, 1, 3), 4), "y": y, "z": z}
+    )
+    turn = (x == 3) & (core == 1)
+    over, back = device(moved(c, "y", 2)), device(moved(c, "y", -2))
 
     def zstep(k):
         return rem(z + jnp.where(core == 0, k + 8, 8 - k), 8)
@@ -101,7 +108,7 @@
         return device(n)
 
     barrier = pltpu.get_barrier_semaphore()
-    peers = [nxt, prv, sibling]
+    peers = [nxt, prv, sibling, across]
     for axis in ("x", "y", "z"):
         for k in range(1, SIZES[axis]):
             peers.append(device(moved(c, axis, k)))
@@ -141,84 +148,128 @@
             return pg.at[pl.ds(pl.multiple_of((w * 2 + b) * BLOCK + h * HALF, HALF), HALF)]
         return pg.at[pl.ds(pl.multiple_of((w * 2 + b) * BLOCK + h * HALF + u * QUARTER, QUARTER), QUARTER)]
 
-    own_half = proj_in.at[pl.ds(pl.multiple_of(core * HALF, HALF), HALF)]
-
     def own_quarter(u):
         return proj_in.at[pl.ds(pl.multiple_of(core * HALF + u * QUARTER, QUARTER), QUARTER)]
 
     zf, zb = zdev(1), zdev(-1)
     yu, yd = device(moved(c, "y", 1)), device(moved(c, "y", -1))
-    go(remote(own_half, prow(z, y_lo, core), gz_send.at[0], gz_recv.at[0], zf))
-    go(remote(own_half, prow(z, y_lo, core), gz_send.at[4], gz_recv.at[4], zb))
-    halo = []
-    for i in range(PIECES):
+    for u in range(2):
+        go(remote(own_quarter(u), prow(z, y_lo, core, u), gz_send.at[u], gz_recv.at[u], zf))
+        go(remote(own_quarter(u), prow(z, y_lo, core, u), gz_send.at[8 + u], gz_recv.at[8 + u], zb))
+    def halo_copy(t, i, to, src=None):
         cols = pl.ds(i * PIECE, PIECE)
-        a = remote(k_in.at[:, cols], kw.at[pl.ds(0, TOK), cols], halo_send.at[i], halo_recv.at[i], nxt)
-        b = remote(
-            v_in.at[:, cols], vw.at[pl.ds(0, TOK), cols], halo_send.at[PIECES + i], halo_recv.at[PIECES + i], nxt
-        )
-        if i == 0:
-            loads[0].wait()
-            go(remote(docs.at[0], docs.at[1], halo_send.at[2 * PIECES], halo_recv.at[2 * PIECES], nxt))
-        go(a)
-        go(b)
-        halo.append((a, b))
-
-    def y_sends(slot, srcs, w):
-        go(remote(srcs[0], prow(w, y_lo, core, 0), gy_send.at[2 * slot], gy_recv.at[2 * slot], yu))
-        go(remote(srcs[1], prow(w, y_lo, core, 1), gy_send.at[2 * slot + 1], gy_recv.at[2 * slot + 1], yd))
-
-    y_sends(0, [own_quarter(0), own_quarter(1)], z)
+        slot = t * PIECES + i
+        at = (kw, vw)[t].at[pl.ds(0, TOK), cols]
+        return remote((k_in, v_in)[t].at[:, cols] if src is None else src, at, halo_send.at[slot], halo_recv.at[slot], to)
+
+    def relay_copy(t, i):
+        cols = pl.ds(i * PIECE, PIECE)
+        slot = t * 2 + i - 2
+        return remote((k_in, v_in)[t].at[:, cols], relay.at[slot], rel_send.at[slot], rel_recv.at[slot], over)
+
+    def pass_on(t, i):
+        return halo_copy(t, i, across, relay.at[t * 2 + i - 2])
+
+    loads[0].wait()
+    docs_copy = go(remote(docs.at[0], docs.at[1], halo_send.at[2 * PIECES], halo_recv.at[2 * PIECES], nxt))
+    for i in range(2):
+        for t in range(2):
+            go(halo_copy(t, i, nxt))
+
+    @pl.when(turn)
+    def _():
+        for i in (2, 3):
+            for t in range(2):
+                relay_copy(t, i).start()
+
+    @pl.when(jnp.logical_not(turn))
+    def _():
+        for i in (2, 3):
+            for t in range(2):
+                halo_copy(t, i, nxt).start()
+
+    def relay_pass(i):
+        @pl.when(turn)
+        def _():
+            for t in range(2):
+                relay_copy(t, i).wait_recv()
+                pass_on(t, i).start()
+
+    def halo_wait(i):
+        for t in range(2):
+            halo_copy(t, i, nxt).wait_recv()
+
+    def halo_sent():
+        @pl.when(turn)
+        def _():
+            for i in (2, 3):
+                for t in range(2):
+                    relay_copy(t, i).wait_send()
+                    pass_on(t, i).wait_send()
+
+        @pl.when(jnp.logical_not(turn))
+        def _():
+            for i in (2, 3):
+                for t in range(2):
+                    halo_copy(t, i, nxt).wait_send()
+
+    ahead = [0, 1, -1, 2, -2, 3, -3, 4]
+
+    def y_way(j, u):
+        return j not in (0, 2) and (j % 2 == 1) == (u == 0)
+
+    def y_send(j, u, src):
+        ref = prow(zstep(-ahead[j]), y_lo, core, u)
+        go(remote(src, ref, gy_send.at[2 * j + u], gy_recv.at[2 * j + u], yu if y_way(j, u) else yd))
+
+    for u in range(2):
+        y_send(0, u, own_quarter(u))
 
     def core_send(slot, w, b):
         ref = prow(w, b, core)
         go(remote(ref, ref, gc_send.at[slot], gc_recv.at[slot], sibling))
 
-    def z_arrival(slot, k):
-        w = zstep(-k)
-        ref = prow(w, y_lo, core)
-        last = slot in (3, 6)
+    def z_arrival(j, u):
+        w = zstep(-ahead[j])
+        ref = prow(w, y_lo, core, u)
+        k = (j - 1) // 2
+        slot = 2 * k + u if j % 2 else 8 + 2 * k + u
         remote(ref, ref, gz_send.at[slot], gz_recv.at[slot], zf).wait_recv()
-        if not last:
-            go(remote(ref, ref, gz_send.at[slot + 1], gz_recv.at[slot + 1], zf if slot < 4 else zb))
-        y_sends(slot + 1, [prow(w, y_lo, core, 0), prow(w, y_lo, core, 1)], w)
-        core_send(slot, w, y_lo)
-
-    def y_arrival(slot, k):
-        w = zstep(-k)
-        for u, frm in ((0, yu), (1, yd)):
+        if j < 6:
+            go(remote(ref, ref, gz_send.at[slot + 2], gz_recv.at[slot + 2], zf if j % 2 else zb))
+        y_send(j, u, ref)
+        if u:
+            core_send(j - 1, w, y_lo)
+
+    def y_arrival(j):
+        w = zstep(-ahead[j])
+        for u in range(2):
             ref = prow(w, 1 - y_lo, core, u)
-            remote(ref, ref, gy_send.at[2 * slot + u], gy_recv.at[2 * slot + u], frm).wait_recv()
-        core_send(7 + slot, w, 1 - y_lo)
-
-    def core_arrival(slot, k, b):
-        ref = prow(zstep(k), b, 1 - core)
+            remote(ref, ref, gy_send.at[2 * j + u], gy_recv.at[2 * j + u], yu).wait_recv()
+        core_send(7 + j, w, 1 - y_lo)
+
+    def core_arrival(slot):
+        w, b = (zstep(ahead[slot + 1]), y_lo) if slot < 7 else (zstep(ahead[slot - 7]), 1 - y_lo)
+        ref = prow(w, b, 1 - core)
         remote(ref, ref, gc_send.at[slot], gc_recv.at[slot], sibling).wait_recv()
 
-    z_order = [(0, 1), (4, -1), (1, 2), (5, -2), (2, 3), (6, -3), (3, 4)]
-    y_order = [(0, 0)] + [(slot + 1, k) for slot, k in z_order]
-
-    remote(docs.at[0], docs.at[1], halo_send.at[2 * PIECES], halo_recv.at[2 * PIECES], nxt).wait_recv()
-    mine = jnp.broadcast_to(docs[0].astype(F32), (TOK, TOK))
-    before = jnp.broadcast_to(docs[1].astype(F32), (TOK, TOK))
-    before = jnp.where(s == 0, -1.0, before)
-    rows = jnp.transpose(mine)
-    causal = lax.broadcasted_iota(jnp.int32, (TOK, TOK), 1) <= lax.broadcasted_iota(jnp.int32, (TOK, TOK), 0)
-    bias[:, TOK:] = jnp.where(causal & (mine == rows), 0.0, -jnp.inf)
-    bias[:, :TOK] = jnp.where(before == rows, 0.0, -jnp.inf)
-
-    ri = lax.broadcasted_iota(jnp.int32, (RANK, 512), 0)
-    ci = lax.broadcasted_iota(jnp.int32, (RANK, 512), 1)
-    want = ((ci & 127) >> 3) * 16 + (ci >> 7) * 4 + (ci & 3)
-    dup[...] = jnp.where(ri == want, 1.0, 0.0).astype(BF)
-    ri = lax.broadcasted_iota(jnp.int32, (512, 512), 0)
-    ci = lax.broadcasted_iota(jnp.int32, (512, 512), 1)
-    want = ((ci & 127) >> 5) * 128 + (ci >> 7) * 32 + (ci & 31)
-    perm[...] = jnp.where(ri == want, 1.0, 0.0).astype(BF)
+    def low_part(w, b, h):
+        at = pl.multiple_of((w * 2 + b) * BLOCK + h * HALF, HALF)
+        return dot_plain(hid[:, pl.ds(at, HALF)], pg[pl.ds(at, HALF)])
+
+    def low_core(slot):
+        w, b = (zstep(ahead[slot + 1]), y_lo) if slot < 7 else (zstep(ahead[slot - 7]), 1 - y_lo)
+        return low_part(w, b, 1 - core)
+
+    def add_low(parts):
+        tot = parts[0]
+        for p in parts[1:]:
+            tot = tot + p
+        acc[...] += tot
 
     score_scale = 1.0 / HD**0.5
 
-    def attend(gi, carry):
+    def attend(gi):
         wide = pl.multiple_of(gi * 512, 512)
         thin = pl.multiple_of(gi * HD, HD)
         qh = [q[:, pl.ds(wide + j * HD, HD)] for j in range(4)]
@@ -239,53 +290,86 @@
         dqv = (dot_plain(ds, kwin) * score_scale).astype(BF)
         for j in range(4):
             dq[:, pl.ds(wide + j * HD, HD)] = dqv[j * TOK : (j + 1) * TOK]
-        dk[:, pl.ds(thin, HD)] = (dot_first(ds, q4) * score_scale).astype(BF)
-        dv[:, pl.ds(thin, HD)] = dot_first(low, g4).astype(BF)
-        return carry
-
-    def halo_wait(i):
-        for cp in halo[i]:
-            cp.wait_recv()
+        dkv[pl.ds(0, 2 * TOK), pl.ds(thin, HD)] = (dot_first(ds, q4) * score_scale).astype(BF)
+        dkv[pl.ds(2 * TOK, 2 * TOK), pl.ds(thin, HD)] = dot_first(low, g4).astype(BF)
+
+    docs_copy.wait_recv()
+    mine = jnp.broadcast_to(docs[0].astype(F32), (TOK, TOK))
+    before = jnp.broadcast_to(docs[1].astype(F32), (TOK, TOK))
+    before = jnp.where(s == 0, -1.0, before)
+    rows = jnp.transpose(mine)
+    causal = lax.broadcasted_iota(jnp.int32, (TOK, TOK), 1) <= lax.broadcasted_iota(jnp.int32, (TOK, TOK), 0)
+    bias[:, TOK:] = jnp.where(causal & (mine == rows), 0.0, -jnp.inf)
+    bias[:, :TOK] = jnp.where(before == rows, 0.0, -jnp.inf)
 
     for cp in loads[1:5]:
         cp.wait()
+    z_arrival(1, 0)
+    z_arrival(2, 0)
     halo_wait(0)
-    lax.fori_loop(0, 2, attend, 0)
-    z_arrival(*z_order[0])
-    z_arrival(*z_order[1])
-    y_arrival(*y_order[0])
+    attend(0)
+    z_arrival(1, 1)
+    z_arrival(2, 1)
+    y_arrival(0)
+    attend(1)
+    relay_pass(2)
+    z_arrival(3, 0)
+    z_arrival(4, 0)
     halo_wait(1)
-    lax.fori_loop(2, 4, attend, 0)
-    z_arrival(*z_order[2])
-    z_arrival(*z_order[3])
-    y_arrival(*y_order[1])
-    y_arrival(*y_order[2])
+    attend(2)
+    relay_pass(3)
+    z_arrival(3, 1)
+    z_arrival(4, 1)
+    y_arrival(1)
+    attend(3)
+    z_arrival(5, 0)
+    z_arrival(6, 0)
+    y_arrival(2)
     halo_wait(2)
-    lax.fori_loop(4, 6, attend, 0)
-    z_arrival(*z_order[4])
-    z_arrival(*z_order[5])
-    y_arrival(*y_order[3])
-    y_arrival(*y_order[4])
+    attend(4)
+    z_arrival(5, 1)
+    z_arrival(6, 1)
+    attend(5)
+    z_arrival(7, 0)
+    y_arrival(3)
     halo_wait(3)
-    lax.fori_loop(6, 8, attend, 0)
-    z_arrival(*z_order[6])
-    for i in range(5, 8):
-        y_arrival(*y_order[i])
-    for slot, k in z_order:
-        core_arrival(slot, k, y_lo)
-    for slot, k in y_order:
-        core_arrival(7 + slot, k, 1 - y_lo)
+    attend(6)
+    z_arrival(7, 1)
+    y_arrival(4)
+    attend(7)
+    y_arrival(5)
+    ri = lax.broadcasted_iota(jnp.int32, (512, RANK), 0)
+    ci = lax.broadcasted_iota(jnp.int32, (512, RANK), 1)
+    want = ((ri & 127) >> 3) * 16 + (ri >> 7) * 4 + (ri & 3)
+    dup[...] = jnp.where(ci == want, 1.0, 0.0).astype(BF)
+    ri = lax.broadcasted_iota(jnp.int32, (512, 512), 0)
+    ci = lax.broadcasted_iota(jnp.int32, (512, 512), 1)
+    want = ((ci & 127) >> 5) * 128 + (ci >> 7) * 32 + (ci & 31)
+    perm[...] = jnp.where(ri == want, 1.0, 0.0).astype(BF)
+
     loads[5].wait()
     loads[6].wait()
-
-    lr[pl.ds(TOK, TOK)] = dot_plain(hid[...], pg[...]).astype(BF)
+    at = pl.multiple_of(d * BLOCK, BLOCK)
+    acc[...] = dot_plain(hid[:, pl.ds(at, BLOCK)], pg[pl.ds(at, BLOCK)])
+    add_low([low_part(zstep(-ahead[j]), y_lo, core) for j in range(1, 8)])
+    y_arrival(6)
+    add_low([low_part(zstep(-ahead[j]), 1 - y_lo, core) for j in range(7)])
+    y_arrival(7)
+    order = [0, 1, 7, 2, 3, 8, 9, 4, 10, 11, 5, 6, 12, 13, 14]
+    add_low([low_part(zstep(-ahead[7]), 1 - y_lo, core)])
+    for some in (order[:9], order[9:13], order[13:]):
+        for slot in some:
+            core_arrival(slot)
+        add_low([low_core(slot) for slot in some])
+
+    lr[pl.ds(TOK, TOK)] = acc[...].astype(BF)
     lr_copy = go(
         remote(lr.at[pl.ds(TOK, TOK)], lr.at[pl.ds(0, TOK)], halo_send.at[2 * PIECES + 1], halo_recv.at[2 * PIECES + 1], nxt)
     )
-    own_lr = lr[pl.ds(TOK, TOK)]
+    turned = jnp.transpose(acc[...]).astype(BF)
 
     def project(gi):
-        part = dot_first(own_lr, dq[:, pl.ds(pl.multiple_of(gi * 512, 512), 512)]).astype(BF)
+        part = dot_plain(turned, dq[:, pl.ds(pl.multiple_of(gi * 512, 512), 512)]).astype(BF)
         for j in range(4):
             piece = part[:, j * HD : (j + 1) * HD].reshape(8, 2, 16, HD)
             at_x = rem(2 * gi + j // 2, 4)
@@ -304,20 +388,6 @@
     qc = [go(remote(zq.at[1 - core, pl.ds(0, 2)], rq.at[pl.ds(0, 2)], rc_send.at[0], rc_recv.at[0], sibling))]
     lax.fori_loop(0, 4, project_odd, 0)
     qc.append(go(remote(zq.at[1 - core, pl.ds(2, 2)], rq.at[pl.ds(2, 2)], rc_send.at[1], rc_recv.at[1], sibling)))
-
-    lr_copy.wait_recv()
-    spread = dot_plain(lr[...], dup[...]).astype(BF)
-    kind = (lax.broadcasted_iota(jnp.int32, (256, 512), 1) >> 2) & 1
-    left_k = jnp.where(kind == 0, spread, jnp.zeros_like(spread))
-    left_v = jnp.where(kind == 1, spread, jnp.zeros_like(spread))
-    for a in range(KVH):
-        cols = slice(a * HD, (a + 1) * HD)
-        both = (dot_first(left_k, dk[:, cols]) + dot_first(left_v, dv[:, cols])).astype(BF)
-        wide = jnp.concatenate([both[i * 128 : (i + 1) * 128] for i in range(4)], axis=1)
-        wide = dot_plain(wide, perm[...]).astype(BF)
-        for b in range(4):
-            zk[b % 2, :, (a % 2) * 2 + b // 2, a // 2] = wide[:, b * HD : (b + 1) * HD].reshape(8, 16, HD)
-    kc = go(remote(zk.at[1 - core], rk, rc_send.at[2], rc_recv.at[2], sibling))
 
     for cp in qc:
         cp.wait_recv()
@@ -327,6 +397,23 @@
         xq[at] = (zq[core, at].astype(F32) + rq[at].astype(F32)).astype(BF)
         if k:
             qx.append(go(remote(xq.at[at], xr.at[k - 1], qx_send.at[k - 1], qx_recv.at[k - 1], device(moved(c, "x", k)))))
+
+    lr_copy.wait_recv()
+    spread = dot_rows(dup[...], lr[...])
+    kind = (lax.broadcasted_iota(jnp.int32, (512, 256), 0) >> 2) & 1
+    left[:, : 2 * TOK] = jnp.where(kind == 0, spread, 0.0).astype(BF)
+    left[:, 2 * TOK :] = jnp.where(kind == 1, spread, 0.0).astype(BF)
+    for a in range(0, KVH, 2):
+        both = dot_plain(left[...], dkv[:, a * HD : (a + 2) * HD]).astype(BF)
+        for t in range(2):
+            wide = jnp.concatenate(
+                [both[i * 128 : (i + 1) * 128, t * HD : (t + 1) * HD] for i in range(4)], axis=1
+            )
+            wide = dot_plain(wide, perm[...]).astype(BF)
+            for b in range(4):
+                zk[b % 2, :, t * 2 + b // 2, a // 2] = wide[:, b * HD : (b + 1) * HD].reshape(8, 16, HD)
+    kc = go(remote(zk.at[1 - core], rk, rc_send.at[2], rc_recv.at[2], sibling))
+
     kc.wait_recv()
     kz = []
     for k in (4, 3, 5, 2, 6, 1, 7, 0):
@@ -392,10 +479,11 @@
     outkv_ref[...] = kv_sum[pl.ds(pl.multiple_of(y_lo * 8, 8), 8)]
     for cp in sent:
         cp.wait_send()
+    halo_sent()
 
 
 def reduced(hid, q, k, v, g, docs, proj):
-    any_spec = pl.BlockSpec(memory_space=pl.ANY)
+    any_spec = pl.BlockSpec(memory_space=pltpu.HBM)
     vmem = pl.BlockSpec(memory_space=pltpu.VMEM)
     dma = pltpu.SemaphoreType.DMA
     halos = 2 * PIECES + 2
@@ -409,10 +497,11 @@
         pltpu.VMEM((TOK, 2 * TOK), F32),
         pltpu.VMEM((DEPTH, RANK), BF),
         pltpu.VMEM((TOK, QCOLS), BF),
-        pltpu.VMEM((2 * TOK, KCOLS), BF),
-        pltpu.VMEM((2 * TOK, KCOLS), BF),
+        pltpu.VMEM((4 * TOK, KCOLS), BF),
+        pltpu.VMEM((TOK, RANK), F32),
         pltpu.VMEM((2 * TOK, RANK), BF),
-        pltpu.VMEM((RANK, 512), BF),
+        pltpu.VMEM((512, 4 * TOK), BF),
+        pltpu.VMEM((512, RANK), BF),
         pltpu.VMEM((512, 512), BF),
         pltpu.VMEM((2, 4, 8, 8, 16, HD), BF),
         pltpu.VMEM((4, 8, 8, 16, HD), BF),
@@ -431,9 +520,10 @@
         pltpu.VMEM((4, 16, HD), BF),
         pltpu.VMEM((7, 16, HD), BF),
         pltpu.VMEM((16, HD), F32),
+        pltpu.VMEM((4, TOK, PIECE), BF),
         dma((7,)),
     ]
-    for n in (halos, 7, 16, 15, 3, 3, 7, 7, 7, 3, 7):
+    for n in (4, halos, 14, 16, 15, 3, 3, 7, 7, 7, 3, 7):
         scratch += [dma((n,)), dma((n,))]
     return pl.pallas_call(
         kernel,
@@ -442,7 +532,7 @@
         out_specs=(vmem, vmem),
         scratch_shapes=scratch,
         compiler_params=pltpu.CompilerParams(
-            collective_id=0, has_side_effects=True, vmem_limit_bytes=48 * 1024 * 1024
+            collective_id=0, has_side_effects=True, vmem_limit_bytes=62 * 1024 * 1024
         ),
         name="backward",
     )(hid, q, k, v, g, docs, proj)

time: 86.3 us -> 75.2 us (0.87)
  local copies, waits for them, and re-layouts: 7.64 us -> 0.77 us
  Pallas kernels: 76.4 us -> 71.6 us
    unnamed x22 -> x8, local copies, waits for them, and re-layouts: 7.55 us -> 0.02 us
    pallas_call x1, Pallas kernels: 76.4 us -> 71.6 us  [reduced(): pl.pallas_call(kernel, out_shape=(jax.ShapeDtypeStruct((16, HD), F32), ja...]
where the time goes in v2:
time: 75.2 us; the launch traced here: 75 us
  Pallas kernels  71.6 us (95%)
  other arithmetic  1.95 us (3%)
  local copies, waits for them, and re-layouts  0.77 us (1%)
    pallas_call x1, Pallas kernels, reduced(): pl.pallas_call(kernel, out_shape=(jax.ShapeDtypeStruct((16, HD), F32), ja...  71.6 us
    div x2, other arithmetic, adam_update(): corrected_first / (jnp.sqrt(corrected_second) + adam_epsilon)  1.95 us

profile of v2, /device:TPU:2, one launch (start us, length us, event | category | flops | bytes accessed | tf_op | source)
XLA Modules:
  0.0 75.0 jit_solution(6347618829484841414)
XLA Ops:
  0.6 0.0 copy-start
  0.6 0.0 copy-start.1
  0.7 0.0 copy-start.2
  0.7 0.0 copy-start.3
  0.7 71.6 %backward.1 = (f32[16,128]{1,0:T(8,128)}, f32[8,128]{1,0:T(8,128)}) custom-call(bf16[128,8192]{1,0:T(8,128)(2,1)} %bitcast.7, bf16[128,4096]{1,0:T(8,128)(2,1)} %bitcast.8, bf16[128,1024]{1,0:T(8,128)(2,1)} %bitcast.10, bf16[128,1024]{1,0:T(8,128)(2,1)} %bitcast.11, bf16[128,4096]{1,0:T(8,128)(2,1)} %bitcast.9, s32[1,128]{1,0:T(1,128)} %doc_in.1, ...), custom_call_target="tpu_custom_call" | custom-call | tf_op jit(solution)/shard_map/backward/pallas_call | solution.py:528
  72.3 0.7 reshape.18
  73.0 0.0 copy-done
  73.0 0.0 copy-done.1
  73.0 0.6 add_divide_fusion
  73.7 0.0 copy-done.2
  73.7 0.0 copy-done.3
  73.7 1.3 %add_divide_fusion.1 = (f32[16,128]{1,0:T(8,128)}, f32[16,128]{1,0:T(8,128)}, f32[16,128]{1,0:T(8,128)}) fusion(f32[16,128]{1,0:T(8,128)} %get-tuple-element.8, f32[16,128]{1,0:T(8,128)S(1)} %copy-done.2, f32[16,128]{1,0:T(8,128)S(1)} %copy-done.3), kind=kLoop, calls=%fused_computation.6 | loop fusion | flops 22528 | bytes 49152 | tf_op jit(solution)/shard_map/div | solution.py:546
  (1 shorter events, 0.0 us)
Async XLA Ops:
  0.6 72.4 %copy-start = (f32[2,16,32]{2,1,0:T(8,128)S(1)}, f32[2,16,32]{2,1,0:T(8,128)}, u32[]{:S(2)}) copy-start(f32[2,16,32]{2,1,0:T(8,128)} %param.21) | copy-start | bytes 12292
  0.6 72.4 %copy-start.1 = (f32[2,16,32]{2,1,0:T(8,128)S(1)}, f32[2,16,32]{2,1,0:T(8,128)}, u32[]{:S(2)}) copy-start(f32[2,16,32]{2,1,0:T(8,128)} %param.20) | copy-start | bytes 12292
  0.7 73.0 %copy-start.2 = (f32[16,128]{1,0:T(8,128)S(1)}, f32[16,128]{1,0:T(8,128)}, u32[]{:S(2)}) copy-start(f32[16,128]{1,0:T(8,128)} %param.19) | copy-start | bytes 24580
  0.7 73.0 %copy-start.3 = (f32[16,128]{1,0:T(8,128)S(1)}, f32[16,128]{1,0:T(8,128)}, u32[]{:S(2)}) copy-start(f32[16,128]{1,0:T(8,128)} %param.18) | copy-start | bytes 24580

commit v3 on v2

--- a/solution.py
+++ b/solution.py
@@ -28,6 +28,7 @@
 BLOCK = 512
 HALF = 256
 QUARTER = 128
+FAR = 6
 
 
 def rem(a, n):
@@ -77,8 +78,10 @@
     hid, q, g, kw, vw, docs, bias, pg, dq, dkv, acc, lr, left, dup, perm,
     zq, rq, xq, xr, yq, yr, wq, wr,
     zk, rk, ck, cr, xk, xkr, yk, ykr, kv_sum,
-    relay,
+    relay, cb, cbr, db, dbr, qb, qbr, qc2, qcr,
     load_sem,
+    by_send, by_recv, bqx_send, bqx_recv,
+    bx_send, bx_recv, bz_send, bz_recv,
     rel_send, rel_recv,
     halo_send, halo_recv,
     gz_send, gz_recv, gy_send, gy_recv, gc_send, gc_recv,
@@ -292,6 +295,15 @@
             dq[:, pl.ds(wide + j * HD, HD)] = dqv[j * TOK : (j + 1) * TOK]
         dkv[pl.ds(0, 2 * TOK), pl.ds(thin, HD)] = (dot_first(ds, q4) * score_scale).astype(BF)
         dkv[pl.ds(2 * TOK, 2 * TOK), pl.ds(thin, HD)] = dot_first(low, g4).astype(BF)
+
+    ri = lax.broadcasted_iota(jnp.int32, (512, RANK), 0)
+    ci = lax.broadcasted_iota(jnp.int32, (512, RANK), 1)
+    want = ((ri & 127) >> 3) * 16 + (ri >> 7) * 4 + (ri & 3)
+    dup[...] = jnp.where(ci == want, 1.0, 0.0).astype(BF)
+    ri = lax.broadcasted_iota(jnp.int32, (512, 512), 0)
+    ci = lax.broadcasted_iota(jnp.int32, (512, 512), 1)
+    want = ((ci & 127) >> 5) * 128 + (ci >> 7) * 32 + (ci & 31)
+    perm[...] = jnp.where(ri == want, 1.0, 0.0).astype(BF)
 
     docs_copy.wait_recv()
     mine = jnp.broadcast_to(docs[0].astype(F32), (TOK, TOK))
@@ -338,15 +350,6 @@
     y_arrival(4)
     attend(7)
     y_arrival(5)
-    ri = lax.broadcasted_iota(jnp.int32, (512, RANK), 0)
-    ci = lax.broadcasted_iota(jnp.int32, (512, RANK), 1)
-    want = ((ri & 127) >> 3) * 16 + (ri >> 7) * 4 + (ri & 3)
-    dup[...] = jnp.where(ci == want, 1.0, 0.0).astype(BF)
-    ri = lax.broadcasted_iota(jnp.int32, (512, 512), 0)
-    ci = lax.broadcasted_iota(jnp.int32, (512, 512), 1)
-    want = ((ci & 127) >> 5) * 128 + (ci >> 7) * 32 + (ci & 31)
-    perm[...] = jnp.where(ri == want, 1.0, 0.0).astype(BF)
-
     loads[5].wait()
     loads[6].wait()
     at = pl.multiple_of(d * BLOCK, BLOCK)
@@ -389,20 +392,37 @@
     lax.fori_loop(0, 4, project_odd, 0)
     qc.append(go(remote(zq.at[1 - core, pl.ds(2, 2)], rq.at[pl.ds(2, 2)], rc_send.at[1], rc_recv.at[1], sibling)))
 
-    for cp in qc:
-        cp.wait_recv()
-    qx = []
-    for k in (2, 1, 3, 0):
-        at = rem(x + k, 4)
-        xq[at] = (zq[core, at].astype(F32) + rq[at].astype(F32)).astype(BF)
-        if k:
-            qx.append(go(remote(xq.at[at], xr.at[k - 1], qx_send.at[k - 1], qx_recv.at[k - 1], device(moved(c, "x", k)))))
-
     lr_copy.wait_recv()
     spread = dot_rows(dup[...], lr[...])
     kind = (lax.broadcasted_iota(jnp.int32, (512, 256), 0) >> 2) & 1
     left[:, : 2 * TOK] = jnp.where(kind == 0, spread, 0.0).astype(BF)
     left[:, 2 * TOK :] = jnp.where(kind == 1, spread, 0.0).astype(BF)
+    def qx_copy(at):
+        slot = rem(at - x + 3, 4)
+        to = device({"core": core, "x": at, "y": y, "z": z})
+        part = (pl.ds(0, 8), pl.ds(0, FAR))
+        return remote(xq.at[(at, *part)], xr.at[(slot, *part)], qx_send.at[slot], qx_recv.at[slot], to)
+
+    def qx_start(at):
+        if at % 2 == 0:
+            qc[at // 2].wait_recv()
+        both_cores = (zq[core, at].astype(F32) + rq[at].astype(F32)).astype(BF)
+        xq[at, :, :FAR] = both_cores[:, :FAR]
+        qb[:, at] = both_cores[:, FAR:]
+
+        @pl.when(x != at)
+        def _():
+            qx_copy(at).start()
+
+    def qx_wait(recv):
+        for k in range(1, 4):
+            cp = qx_copy(rem(x + k, 4))
+            if recv:
+                cp.wait_recv()
+            else:
+                cp.wait_send()
+
+    kc = []
     for a in range(0, KVH, 2):
         both = dot_plain(left[...], dkv[:, a * HD : (a + 2) * HD]).astype(BF)
         for t in range(2):
@@ -411,28 +431,64 @@
             )
             wide = dot_plain(wide, perm[...]).astype(BF)
             for b in range(4):
-                zk[b % 2, :, t * 2 + b // 2, a // 2] = wide[:, b * HD : (b + 1) * HD].reshape(8, 16, HD)
-    kc = go(remote(zk.at[1 - core], rk, rc_send.at[2], rc_recv.at[2], sibling))
-
-    kc.wait_recv()
+                zk[b % 2, a // 2, :, t * 2 + b // 2] = wide[:, b * HD : (b + 1) * HD].reshape(8, 16, HD)
+        yh = a // 2
+        kc.append(go(remote(zk.at[1 - core, yh], rk.at[yh], rc_send.at[2 + yh], rc_recv.at[2 + yh], sibling)))
+        if a < 4:
+            qx_start(a)
+            qx_start(a + 1)
+
+    by = []
+    for k in (4, 3, 5, 2, 6, 1, 7):
+        at = rem(y + k, 8)
+        by.append(go(remote(qb.at[at], qbr.at[k - 1], by_send.at[k - 1], by_recv.at[k - 1], device(moved(c, "y", k)))))
+    for yh in range(2):
+        kc[yh].wait_recv()
+        ck[:, :, yh] = (zk[core, yh].astype(F32) + rk[yh].astype(F32)).astype(BF)
     kz = []
-    for k in (4, 3, 5, 2, 6, 1, 7, 0):
+    for k in (4, 3, 5, 2, 6, 1, 7):
         at = rem(z + k, 8)
-        ck[at] = (zk[core, at].astype(F32) + rk[at].astype(F32)).astype(BF)
-        if k:
-            kz.append(go(remote(ck.at[at], cr.at[k - 1], kz_send.at[k - 1], kz_recv.at[k - 1], device(moved(c, "z", k)))))
-
-    for cp in qx:
-        cp.wait_recv()
+        kz.append(go(remote(ck.at[at], cr.at[k - 1], kz_send.at[k - 1], kz_recv.at[k - 1], device(moved(c, "z", k)))))
+    for yh in range(2):
+        kc[2 + yh].wait_recv()
+        for at in range(4):
+            cb[at, :, yh] = (zk[core, 2 + yh, :, at].astype(F32) + rk[2 + yh, :, at].astype(F32)).astype(BF)
+    bx = []
+    for k in (2, 1, 3):
+        at = rem(x + k, 4)
+        bx.append(go(remote(cb.at[at], cbr.at[k - 1], bx_send.at[k - 1], bx_recv.at[k - 1], device(moved(c, "x", k)))))
+
+    qx_wait(True)
     qy = []
     for k in (4, 3, 5, 2, 6, 1, 7, 0):
         at = rem(y + k, 8)
-        tot = xq[x, at].astype(F32)
+        tot = xq[x, at, :FAR].astype(F32)
         for i in range(3):
-            tot = tot + xr[i, at].astype(F32)
+            tot = tot + xr[i, at, :FAR].astype(F32)
         yq[at] = tot.astype(BF)
         if k:
             qy.append(go(remote(yq.at[at], yr.at[k - 1], qy_send.at[k - 1], qy_recv.at[k - 1], device(moved(c, "y", k)))))
+    for cp in by:
+        cp.wait_recv()
+    bqx = []
+    for k in (2, 1, 3, 0):
+        at = rem(x + k, 4)
+        tot = qb[y, at].astype(F32)
+        for i in range(7):
+            tot = tot + qbr[i, at].astype(F32)
+        qc2[at] = tot.astype(BF)
+        if k:
+            bqx.append(go(remote(qc2.at[at], qcr.at[k - 1], bqx_send.at[k - 1], bqx_recv.at[k - 1], device(moved(c, "x", k)))))
+    for cp in bx:
+        cp.wait_recv()
+    bz = []
+    tot = cb[x].astype(F32)
+    for i in range(3):
+        tot = tot + cbr[i].astype(F32)
+    db[...] = tot.astype(BF)
+    for k in (4, 3, 5, 2, 6, 1, 7):
+        at = rem(z + k, 8)
+        bz.append(go(remote(db.at[at], dbr.at[k - 1], bz_send.at[k - 1], bz_recv.at[k - 1], device(moved(c, "z", k)))))
     for cp in kz:
         cp.wait_recv()
     kx = []
@@ -449,17 +505,29 @@
     tot = yq[y].astype(F32)
     for i in range(7):
         tot = tot + yr[i].astype(F32)
-    wq[...] = tot.astype(BF)
+    wq[pl.ds(0, FAR)] = tot.astype(BF)
+    for cp in bqx:
+        cp.wait_recv()
+    tot = qc2[x].astype(F32)
+    for i in range(3):
+        tot = tot + qcr[i].astype(F32)
+    wq[pl.ds(FAR, 8 - FAR)] = tot.astype(BF)
     qz = []
     for k in (4, 3, 5, 2, 6, 1, 7):
         at = rem(z + k, 8)
         qz.append(go(remote(wq.at[at], wr.at[k - 1], qz_send.at[k - 1], qz_recv.at[k - 1], device(moved(c, "z", k)))))
+    for cp in bz:
+        cp.wait_recv()
+    tot = db[z].astype(F32)
+    for i in range(7):
+        tot = tot + dbr[i].astype(F32)
+    yk[pl.ds(2, 2)] = tot.astype(BF)
     for cp in kx:
         cp.wait_recv()
     tot = xk[x].astype(F32)
     for i in range(3):
         tot = tot + xkr[i].astype(F32)
-    yk[...] = tot.astype(BF)
+    yk[pl.ds(0, 2)] = tot.astype(BF)
     ky = []
     for k in (4, 3, 5, 2, 6, 1, 7):
         to = moved(c, "y", k)
@@ -480,6 +548,7 @@
     for cp in sent:
         cp.wait_send()
     halo_sent()
+    qx_wait(False)
 
 
 def reduced(hid, q, k, v, g, docs, proj):
@@ -507,23 +576,31 @@
         pltpu.VMEM((4, 8, 8, 16, HD), BF),
         pltpu.VMEM((4, 8, 8, 16, HD), BF),
         pltpu.VMEM((3, 8, 8, 16, HD), BF),
-        pltpu.VMEM((8, 8, 16, HD), BF),
-        pltpu.VMEM((7, 8, 16, HD), BF),
+        pltpu.VMEM((8, FAR, 16, HD), BF),
+        pltpu.VMEM((7, FAR, 16, HD), BF),
         pltpu.VMEM((8, 16, HD), BF),
         pltpu.VMEM((7, 16, HD), BF),
-        pltpu.VMEM((2, 8, 4, 4, 16, HD), BF),
-        pltpu.VMEM((8, 4, 4, 16, HD), BF),
-        pltpu.VMEM((8, 4, 4, 16, HD), BF),
-        pltpu.VMEM((7, 4, 4, 16, HD), BF),
-        pltpu.VMEM((4, 4, 16, HD), BF),
-        pltpu.VMEM((3, 4, 16, HD), BF),
+        pltpu.VMEM((2, 4, 8, 4, 16, HD), BF),
+        pltpu.VMEM((4, 8, 4, 16, HD), BF),
+        pltpu.VMEM((8, 4, 2, 16, HD), BF),
+        pltpu.VMEM((7, 4, 2, 16, HD), BF),
+        pltpu.VMEM((4, 2, 16, HD), BF),
+        pltpu.VMEM((3, 2, 16, HD), BF),
         pltpu.VMEM((4, 16, HD), BF),
         pltpu.VMEM((7, 16, HD), BF),
         pltpu.VMEM((16, HD), F32),
         pltpu.VMEM((4, TOK, PIECE), BF),
+        pltpu.VMEM((4, 8, 2, 16, HD), BF),
+        pltpu.VMEM((3, 8, 2, 16, HD), BF),
+        pltpu.VMEM((8, 2, 16, HD), BF),
+        pltpu.VMEM((7, 2, 16, HD), BF),
+        pltpu.VMEM((8, 4, 8 - FAR, 16, HD), BF),
+        pltpu.VMEM((7, 4, 8 - FAR, 16, HD), BF),
+        pltpu.VMEM((4, 8 - FAR, 16, HD), BF),
+        pltpu.VMEM((3, 8 - FAR, 16, HD), BF),
         dma((7,)),
     ]
-    for n in (4, halos, 14, 16, 15, 3, 3, 7, 7, 7, 3, 7):
+    for n in (7, 3, 3, 7, 4, halos, 14, 16, 15, 6, 3, 7, 7, 7, 3, 7):
         scratch += [dma((n,)), dma((n,))]
     return pl.pallas_call(
         kernel,

time: 75.2 us -> 73.3 us (0.975)
  Pallas kernels: 71.6 us -> 69.6 us
    pallas_call x1, Pallas kernels: 71.6 us -> 69.6 us  [reduced(): pl.pallas_call(kernel, out_shape=(jax.ShapeDtypeStruct((16, HD), F32), ja...]
where the time goes in v3:
time: 73.3 us; the launch traced here: 73 us
  Pallas kernels  69.6 us (95%)
  other arithmetic  1.95 us (3%)
  local copies, waits for them, and re-layouts  0.77 us (1%)
    pallas_call x1, Pallas kernels, reduced(): pl.pallas_call(kernel, out_shape=(jax.ShapeDtypeStruct((16, HD), F32), ja...  69.6 us
    div x2, other arithmetic, adam_update(): corrected_first / (jnp.sqrt(corrected_second) + adam_epsilon)  1.95 us

profile of v3, /device:TPU:2, one launch (start us, length us, event | category | flops | bytes accessed | tf_op | source)
XLA Modules:
  0.0 73.0 jit_solution(1594244218807101341)
XLA Ops:
  0.6 0.0 copy-start
  0.6 0.0 copy-start.1
  0.7 0.0 copy-start.2
  0.7 0.0 copy-start.3
  0.7 69.6 %backward.1 = (f32[16,128]{1,0:T(8,128)}, f32[8,128]{1,0:T(8,128)}) custom-call(bf16[128,8192]{1,0:T(8,128)(2,1)} %bitcast.7, bf16[128,4096]{1,0:T(8,128)(2,1)} %bitcast.8, bf16[128,1024]{1,0:T(8,128)(2,1)} %bitcast.10, bf16[128,1024]{1,0:T(8,128)(2,1)} %bitcast.11, bf16[128,4096]{1,0:T(8,128)(2,1)} %bitcast.9, s32[1,128]{1,0:T(1,128)} %doc_in.1, ...), custom_call_target="tpu_custom_call" | custom-call | tf_op jit(solution)/shard_map/backward/pallas_call | solution.py:605
  70.3 0.7 %reshape.18 = f32[2,4,4,32]{3,2,1,0:T(4,128)S(1)} reshape(f32[8,128]{1,0:T(8,128)} %get-tuple-element.9) | data formatting | bytes 8192 | tf_op jit(solution)/shard_map/reshape | solution.py:632
  71.1 0.0 copy-done
  71.1 0.0 copy-done.1
  71.1 0.6 add_divide_fusion
  71.7 0.0 copy-done.2
  71.7 0.0 copy-done.3
  71.7 1.3 %add_divide_fusion.1 = (f32[16,128]{1,0:T(8,128)}, f32[16,128]{1,0:T(8,128)}, f32[16,128]{1,0:T(8,128)}) fusion(f32[16,128]{1,0:T(8,128)} %get-tuple-element.8, f32[16,128]{1,0:T(8,128)S(1)} %copy-done.2, f32[16,128]{1,0:T(8,128)S(1)} %copy-done.3), kind=kLoop, calls=%fused_computation.6 | loop fusion | flops 22528 | bytes 49152 | tf_op jit(solution)/shard_map/div | solution.py:623
  (1 shorter events, 0.0 us)
Async XLA Ops:
  0.6 70.4 %copy-start = (f32[2,16,32]{2,1,0:T(8,128)S(1)}, f32[2,16,32]{2,1,0:T(8,128)}, u32[]{:S(2)}) copy-start(f32[2,16,32]{2,1,0:T(8,128)} %param.21) | copy-start | bytes 12292
  0.6 70.4 %copy-start.1 = (f32[2,16,32]{2,1,0:T(8,128)S(1)}, f32[2,16,32]{2,1,0:T(8,128)}, u32[]{:S(2)}) copy-start(f32[2,16,32]{2,1,0:T(8,128)} %param.20) | copy-start | bytes 12292
  0.7 71.1 %copy-start.2 = (f32[16,128]{1,0:T(8,128)S(1)}, f32[16,128]{1,0:T(8,128)}, u32[]{:S(2)}) copy-start(f32[16,128]{1,0:T(8,128)} %param.19) | copy-start | bytes 24580
  0.7 71.1 %copy-start.3 = (f32[16,128]{1,0:T(8,128)S(1)}, f32[16,128]{1,0:T(8,128)}, u32[]{:S(2)}) copy-start(f32[16,128]{1,0:T(8,128)} %param.18) | copy-start | bytes 24580

commit v4 on v3

--- a/solution.py
+++ b/solution.py
@@ -28,7 +28,7 @@
 BLOCK = 512
 HALF = 256
 QUARTER = 128
-FAR = 6
+FAR = 5
 
 
 def rem(a, n):

time: 73.3 us -> 73.7 us (level)
  the two profiles are of different devices: /device:TPU:2 before, /device:TPU:8 now
where the time goes in v4:
time: 73.7 us; the launch traced here: 73.5 us
  Pallas kernels  70.1 us (95%)
  other arithmetic  1.95 us (3%)
  local copies, waits for them, and re-layouts  0.77 us (1%)
    pallas_call x1, Pallas kernels, reduced(): pl.pallas_call(kernel, out_shape=(jax.ShapeDtypeStruct((16, HD), F32), ja...  70.1 us
    div x2, other arithmetic, adam_update(): corrected_first / (jnp.sqrt(corrected_second) + adam_epsilon)  1.95 us

profile of v4, /device:TPU:8, one launch (start us, length us, event | category | flops | bytes accessed | tf_op | source)
XLA Modules:
  0.0 73.5 jit_solution(8523016113216702972)
XLA Ops:
  0.6 0.0 copy-start
  0.6 0.0 copy-start.1
  0.7 0.0 copy-start.2
  0.7 0.0 copy-start.3
  0.7 70.1 %backward.1 = (f32[16,128]{1,0:T(8,128)}, f32[8,128]{1,0:T(8,128)}) custom-call(bf16[128,8192]{1,0:T(8,128)(2,1)} %bitcast.7, bf16[128,4096]{1,0:T(8,128)(2,1)} %bitcast.8, bf16[128,1024]{1,0:T(8,128)(2,1)} %bitcast.10, bf16[128,1024]{1,0:T(8,128)(2,1)} %bitcast.11, bf16[128,4096]{1,0:T(8,128)(2,1)} %bitcast.9, s32[1,128]{1,0:T(1,128)} %doc_in.1, ...), custom_call_target="tpu_custom_call" | custom-call | tf_op jit(solution)/shard_map/backward/pallas_call | solution.py:605
  70.8 0.7 %reshape.18 = f32[2,4,4,32]{3,2,1,0:T(4,128)S(1)} reshape(f32[8,128]{1,0:T(8,128)} %get-tuple-element.9) | data formatting | bytes 8192 | tf_op jit(solution)/shard_map/reshape | solution.py:632
  71.5 0.0 copy-done
  71.5 0.0 copy-done.1
  71.6 0.6 add_divide_fusion
  72.2 0.0 copy-done.2
  72.2 0.0 copy-done.3
  72.2 1.3 %add_divide_fusion.1 = (f32[16,128]{1,0:T(8,128)}, f32[16,128]{1,0:T(8,128)}, f32[16,128]{1,0:T(8,128)}) fusion(f32[16,128]{1,0:T(8,128)} %get-tuple-element.8, f32[16,128]{1,0:T(8,128)S(1)} %copy-done.2, f32[16,128]{1,0:T(8,128)S(1)} %copy-done.3), kind=kLoop, calls=%fused_computation.6 | loop fusion | flops 22528 | bytes 49152 | tf_op jit(solution)/shard_map/div | solution.py:623
  (1 shorter events, 0.0 us)
Async XLA Ops:
  0.6 70.9 %copy-start = (f32[2,16,32]{2,1,0:T(8,128)S(1)}, f32[2,16,32]{2,1,0:T(8,128)}, u32[]{:S(2)}) copy-start(f32[2,16,32]{2,1,0:T(8,128)} %param.21) | copy-start | bytes 12292
  0.6 70.9 %copy-start.1 = (f32[2,16,32]{2,1,0:T(8,128)S(1)}, f32[2,16,32]{2,1,0:T(8,128)}, u32[]{:S(2)}) copy-start(f32[2,16,32]{2,1,0:T(8,128)} %param.20) | copy-start | bytes 12292
  0.7 71.5 %copy-start.2 = (f32[16,128]{1,0:T(8,128)S(1)}, f32[16,128]{1,0:T(8,128)}, u32[]{:S(2)}) copy-start(f32[16,128]{1,0:T(8,128)} %param.19) | copy-start | bytes 24580
  0.7 71.5 %copy-start.3 = (f32[16,128]{1,0:T(8,128)S(1)}, f32[16,128]{1,0:T(8,128)}, u32[]{:S(2)}) copy-start(f32[16,128]{1,0:T(8,128)} %param.18) | copy-start | bytes 24580
